TPU v7x, 128 devices: a whole 4x4x4 slice. The times are simulated.
128 devices in a mesh: section: 2 (over core), expert: 16 (over z, x), shard: 4 (over y).
Axes of the slice: x: 4, y: 4, z: 4, core: 2. Of those that a mesh axis runs over, the one named last changes fastest.
Arguments:
- ends_in: bfloat16 [2, 2, 4096, 1024], P('section', None, ('expert', 'shard')), may hold values from -6 to 6
- segments: int32 [2, 4096], P(None, 'expert'), may hold values from 0 to 4, as said below
- routes: int32 [2, 2, 4096, 8], P('section', None, ('expert', 'shard')), may hold values from 0 to 31, all different within a row; in each aligned block of 64 rows (0 to 63, 64 to 127, ..., all dimensions but the last counted through in order) at most 24 rows name the same one
- gates: float32 [2, 2, 4096, 8], P('section', None, ('expert', 'shard')), may hold values from 0.2 to 0.6
- attn_gain: float32 [2, 1024], P('section'), may hold values from 0.1 to 1.9
- query_gain: float32 [2, 64], P('section'), may hold values from 0.1 to 1.9
- key_gain: float32 [2, 64], P('section'), may hold values from 0.1 to 1.9
- feed_gain: float32 [2, 1024], P('section'), may hold values from 0.1 to 1.9
- w_query: bfloat16 [2, 1024, 1024], P('section', 'expert', 'shard'), may hold values from -0.1875 to 0.1875
- key_weight: bfloat16 [2, 1024, 512], P('section', 'expert', 'shard'), may hold values from -0.1875 to 0.1875
- value_weight: bfloat16 [2, 1024, 512], P('section', 'expert', 'shard'), may hold values from -0.1875 to 0.1875
- w_out: bfloat16 [2, 1024, 1024], P('section', 'shard', 'expert'), may hold values from -1 to 1
- w_gate: bfloat16 [2, 32, 1024, 512], P('section', 'expert'), may hold values from -0.1875 to 0.1875
- w_up: bfloat16 [2, 32, 1024, 512], P('section', 'expert'), may hold values from -0.1875 to 0.1875
- w_down: bfloat16 [2, 32, 512, 1024], P('section', 'expert'), may hold values from -0.5 to 0.5
Outputs:
- ends: bfloat16 [2, 2, 4096, 1024], P('section', None, ('expert', 'shard'))
- grad_attn_gain: float32 [2, 1024], P('section')
- grad_query_gain: float32 [2, 64], P('section')
- grad_key_gain: float32 [2, 64], P('section')
- grad_feed_gain: float32 [2, 1024], P('section')
- grad_w_query: float32 [2, 1024, 1024], P('section', 'expert', 'shard')
- grad_w_key: float32 [2, 1024, 512], P('section', 'expert', 'shard')
- grad_w_value: float32 [2, 1024, 512], P('section', 'expert', 'shard')
- grad_w_out: float32 [2, 1024, 1024], P('section', 'shard', 'expert')
- grad_w_gate: float32 [2, 32, 1024, 512], P('section', 'expert', None, 'shard')
- grad_w_up: float32 [2, 32, 1024, 512], P('section', 'expert', None, 'shard')
- grad_w_down: float32 [2, 32, 512, 1024], P('section', 'expert', 'shard')
Inputs may be any that keep to these rules, and one draw needn't show every extreme that they name: `segments`: within each sequence of 256 consecutive tokens the numbers start at 0 and never fall; a new document begins only within the first or the last 64 tokens of a sequence. `routes`: each row names 8 different experts; in the rows of one device in one micro-batch (aligned blocks of 64 rows) no expert is named more than 24 times.
All inputs are finite; a program needn't handle non-finite values.
Results may differ from a plain program's by a relative error of at most 0.04.
Values may be sent and summed in bfloat16 or wider, within the bound.
A program may use at most 192 MiB of HBM per device.

v0:
```python
import functools

import jax
import jax.numpy as jnp
from jax import lax
from jax.experimental import pallas as pl
from jax.experimental.pallas import tpu as pltpu
from jax.sharding import PartitionSpec as P

EPS = 1e-06
NEG = -1e30
HEAD = 64
RING = 4
MESH = pl.DeviceIdType.MESH
F32 = jnp.float32
BF16 = jnp.bfloat16

NN = (((1,), (0,)), ((), ()))
NT = (((1,), (1,)), ((), ()))
TN = (((0,), (0,)), ((), ()))

(
    Y_GATHER,
    Y_SUM,
    Y_GATHER_BACK,
    Y_SUM_BACK,
    TOKENS,
    TOKENS_BACK,
    PACKED,
    _packed_next,
    PACKED_BACK,
    _packed_back_next,
    RESULT,
    _result_next,
    RESULT_BACK,
    _result_back_next,
    PARTIAL,
    PARTIAL_BACK,
    GRAD_Q,
    _grad_q_next,
    GAIN_P,
    GAIN_Q,
    GAIN_Y,
    WEIGHT_P,
    _weight_p_next,
    TABLE_P,
    RING_ROWS,
) = range(25)

(
    C_ENDS,
    C_GAINS,
    C_ROUTES,
    C_GATES,
    C_PIECE,
    C_HALF,
    _half_next,
    C_GATE,
    C_UP,
    C_DOWN,
    C_GRAD,
    _grad_next,
    _grad_last,
    C_PROJ,
    C_TERM,
    C_OUT_EXPERT,
    _out_expert_next,
    C_OUT_PROJ,
    _out_proj_next,
    C_OUT_ENDS,
    CORE_ROWS,
) = range(21)


def dot(a, b, form=NN):
    return lax.dot_general(a, b, form, preferred_element_type=F32)


def exact_dot(a, b, form=NN):
    return lax.dot_general(
        a, b, form, preferred_element_type=F32, precision=lax.Precision.HIGHEST
    )


def iota(shape, dimension):
    return lax.broadcasted_iota(jnp.int32, shape, dimension)


def swap_heads():
    size = 4 * HEAD
    row, col = iota((size, size), 0), iota((size, size), 1)
    head = lax.div(row, HEAD)
    shift = jnp.where(head == 1, HEAD, jnp.where(head == 2, -HEAD, 0))
    return (col == row + shift).astype(F32)


def copies_of_head(count):
    shape = (HEAD, count * HEAD)
    return (lax.rem(iota(shape, 1), HEAD) == iota(shape, 0)).astype(F32)


def scale_of(rows):
    return lax.rsqrt(jnp.mean(rows * rows, axis=-1, keepdims=True) + EPS)


def kernel(
    rows,
    width,
    hidden,
    capacity,
    ends_ref,
    segments_ref,
    routes_ref,
    gates_ref,
    attn_gain_ref,
    query_gain_ref,
    key_gain_ref,
    feed_gain_ref,
    query_ref,
    key_ref,
    value_ref,
    out_ref,
    gate_ref,
    up_ref,
    down_ref,
    ends_out,
    gains_out,
    proj_out,
    expert_out,
    w_gate,
    w_up,
    w_down,
    w_attn,
    ends_in,
    gains,
    routes,
    gates,
    mask_ref,
    piece_ref,
    gains_ref,
    table_send,
    table_recv,
    slots,
    weights,
    stream,
    middle,
    cotangent,
    attn_all,
    raw_qk,
    values,
    mixed,
    y_send,
    y_recv,
    tokens,
    tokens_back,
    packed_send,
    packed,
    packed_back,
    result_send,
    result,
    result_back_send,
    result_back,
    partial_send,
    partial,
    partial_back,
    parts,
    slopes,
    attn_back,
    back_qk,
    back_v,
    acts,
    grads,
    grads_core,
    grads_y,
    out_stage,
    proj,
    proj_core,
    proj_recv,
    proj_sum,
    proj_last,
    proj_stage,
    terms,
    terms_core,
    terms_recv,
    ends_stage,
    send_sem,
    recv_sem,
    w_send,
    w_recv,
    j_send,
    j_recv,
    g_send,
    g_recv,
    c_send,
    c_recv,
    local_sem,
    out_sem,
    credit,
    y_credit,
):
    core = lax.axis_index("section")
    place = lax.axis_index("expert")
    shard = lax.axis_index("shard")
    x = lax.rem(place, RING)
    z = lax.div(place, RING)
    p = x + core * (z - x)
    q = z + core * (x - z)
    span = RING * rows
    group = RING * capacity
    other = 1 - core

    def mod(value):
        return lax.rem(value + 2 * RING, RING)

    def place_of(second, first):
        return (1 - core) * (second * RING + first) + core * (first * RING + second)

    def y_device(d):
        return (core, place, mod(shard + d))

    def p_device(d):
        return (core, place_of(q, mod(p + d)), shard)

    def q_device(d):
        return (core, place_of(mod(q + d), p), shard)

    core_device = (other, place, shard)

    def ring_copy(row, d, src, dst, device):
        return pltpu.make_async_remote_copy(
            src_ref=src,
            dst_ref=dst,
            send_sem=send_sem.at[row, d - 1],
            recv_sem=recv_sem.at[row, d - 1],
            device_id=device,
            device_id_type=MESH,
        )

    def core_copy(row, src, dst):
        return pltpu.make_async_remote_copy(
            src_ref=src,
            dst_ref=dst,
            send_sem=c_send.at[row],
            recv_sem=c_recv.at[row],
            device_id=core_device,
            device_id_type=MESH,
        )

    barrier = pltpu.get_barrier_semaphore()
    for d in (1, 2, 3):
        for device in (y_device(d), p_device(d), q_device(d)):
            pl.semaphore_signal(barrier, inc=1, device_id=device, device_id_type=MESH)
    pl.semaphore_signal(barrier, inc=1, device_id=core_device, device_id_type=MESH)
    pl.semaphore_wait(barrier, 10)

    swap = swap_heads().astype(BF16)
    piece_ref[0, :, : 4 * HEAD] = dot(query_ref[...], swap).astype(BF16)
    piece_ref[0, :, 4 * HEAD :] = key_ref[...]
    piece_ref[1, :, : 2 * HEAD] = value_ref[...]
    piece_ref[1, :, 2 * HEAD :] = dot(out_ref[...], swap).astype(BF16)
    gains_ref[0:1] = attn_gain_ref[...]
    gains_ref[1:2] = feed_gain_ref[...]
    gains_ref[2:3, : 4 * HEAD] = exact_dot(query_gain_ref[...], copies_of_head(4))
    gains_ref[2:3, 4 * HEAD : 6 * HEAD] = exact_dot(key_gain_ref[...], copies_of_head(2))
    piece_copy = core_copy(C_PIECE, piece_ref.at[other], w_attn.at[core, other, place])
    ends_copy = core_copy(C_ENDS, ends_ref.at[other], ends_in)
    gains_copy = core_copy(C_GAINS, gains_ref, gains.at[core])
    routes_copy = core_copy(C_ROUTES, routes_ref.at[other], routes.at[core])
    gates_copy = core_copy(C_GATES, gates_ref.at[other], gates.at[core])
    for copy in (piece_copy, ends_copy, gains_copy, routes_copy, gates_copy):
        copy.start()
    w_attn[core, core, place] = piece_ref[core]
    gains[core] = gains_ref[...]
    routes[core] = routes_ref[core]
    gates[core] = gates_ref[core]

    def local_weights():
        return (
            pltpu.make_async_copy(gate_ref, w_gate.at[core], local_sem.at[0]),
            pltpu.make_async_copy(up_ref, w_up.at[core], local_sem.at[1]),
            pltpu.make_async_copy(down_ref, w_down.at[core], local_sem.at[2]),
        )

    def sent_weights():
        return (
            core_copy(C_GATE, gate_ref, w_gate.at[core]),
            core_copy(C_UP, up_ref, w_up.at[core]),
            core_copy(C_DOWN, down_ref, w_down.at[core]),
        )

    for copy in local_weights():
        copy.start()

    def weight_first(layer, d):
        return pltpu.make_async_remote_copy(
            src_ref=w_attn.at[layer, core, place],
            dst_ref=w_attn.at[layer, core, place],
            send_sem=send_sem.at[WEIGHT_P + layer, d - 1],
            recv_sem=recv_sem.at[WEIGHT_P + layer, d - 1],
            device_id=p_device(d),
            device_id_type=MESH,
        )

    def weight_second(layer, d, i):
        held = place_of(q, mod(p - i))
        return pltpu.make_async_remote_copy(
            src_ref=w_attn.at[layer, core, held],
            dst_ref=w_attn.at[layer, core, held],
            send_sem=w_send.at[layer, d - 1, i],
            recv_sem=w_recv.at[layer, d - 1, i],
            device_id=q_device(d),
            device_id_type=MESH,
        )

    def weight_half(layer):
        return core_copy(C_HALF + layer, w_attn.at[layer, core], w_attn.at[layer, core])

    def start_first(layer):
        for d in (1, 3, 2):
            weight_first(layer, d).start()

    def start_second(layer):
        for i in (0, 1, 3, 2):
            if i:
                weight_first(layer, i).wait_recv()
            for d in (1, 3, 2):
                weight_second(layer, d, i).start()

    def start_half(layer):
        for i in (0, 1, 3, 2):
            for d in (1, 3, 2):
                weight_second(layer, d, i).wait_recv()
        weight_half(layer).start()

    piece_copy.wait_recv()
    start_first(0)
    start_first(1)
    ends_copy.wait_recv()
    gains_copy.wait_recv()
    first = core == 0
    stream[0] = jnp.where(first, ends_ref[0], ends_in[...]).astype(F32)
    cotangent[...] = jnp.where(first, ends_in[...], ends_ref[1]).astype(F32)

    def make_tables():
        routes_copy.wait_recv()
        gates_copy.wait_recv()
        tiles = 32
        names = iota((tiles, rows), 0)
        ahead = (iota((rows, rows), 0) < iota((rows, rows), 1)).astype(BF16)
        spread = (iota((rows, span), 1) == iota((rows, span), 0) + rows * p).astype(F32)
        row_at = lax.broadcasted_iota(jnp.int32, (2 * RING, tiles), 0)
        col_at = lax.broadcasted_iota(jnp.int32, (2 * RING, tiles), 1)
        for layer in range(2):
            named = jnp.zeros((tiles, rows), F32)
            gate = jnp.zeros((tiles, rows), F32)
            for j in range(routes.shape[1]):
                hit = (routes[layer, j : j + 1, :] == names).astype(F32)
                named = named + hit
                gate = gate + hit * gates[layer, j : j + 1, :]
            rank = dot(named.astype(BF16), ahead)
            slot = named * (rank + (1 + capacity * p).astype(F32))
            wide_slot = exact_dot(slot, spread)
            wide_gate = exact_dot(gate, spread)
            for d in range(RING):
                first_axis = mod(p + d)
                owner = place_of(lax.div(row_at, 2), first_axis)
                choose = (col_at == 2 * owner + lax.rem(row_at, 2)).astype(F32)
                table_send[d, layer, 0] = exact_dot(choose, wide_slot)
                table_send[d, layer, 1] = exact_dot(choose, wide_gate)
        for d in (1, 3, 2):
            ring_copy(
                TABLE_P, d, table_send.at[d], table_recv.at[d - 1], p_device(d)
            ).start()

    def take_tables():
        for d in (1, 3, 2):
            ring_copy(
                TABLE_P, d, table_send.at[d], table_recv.at[d - 1], p_device(d)
            ).wait_recv()
        for layer in range(2):
            for kind, target in ((0, slots), (1, weights)):
                whole = table_send[0, layer, kind]
                for d in (1, 2, 3):
                    whole = whole + table_recv[d - 1, layer, kind]
                for r in range(2 * RING):
                    target[layer, r] = whole[r : r + 1, :]

    def choose_rows(layer, second, f):
        at = lax.broadcasted_iota(jnp.int32, (group, span), 0).astype(F32) + 1.0
        return at == slots[layer, 2 * second + f]

    lanes = lax.broadcasted_iota(jnp.int32, (1, 2 * HEAD), 1)
    low_half = lanes < HEAD
    halves = (low_half, lanes >= HEAD)

    def head_mean(block):
        at_row = lax.broadcasted_iota(jnp.int32, (2 * HEAD, 2 * HEAD), 0) >= HEAD
        at_col = lax.broadcasted_iota(jnp.int32, (2 * HEAD, 2 * HEAD), 1) >= HEAD
        share = jnp.where(at_row == at_col, 1.0 / HEAD, 0.0).astype(F32)
        tiles = [
            exact_dot(block[:, i : i + 2 * HEAD], share)
            for i in range(0, block.shape[1], 2 * HEAD)
        ]
        return jnp.concatenate(tiles, axis=1)

    def qk_gain(layer):
        return gains[layer, 2:3, : 6 * HEAD]

    def make_mask():
        across = jnp.broadcast_to(
            jnp.where(core == 0, segments_ref[0:1], segments_ref[1:2]), (span, span)
        ).astype(F32)
        causal = iota((span, span), 0) >= iota((span, span), 1)
        mask_ref[...] = (causal & (across == across.T)).astype(F32)

    def allowed():
        return mask_ref[...] != 0.0

    def normed_qk(layer):
        raw = raw_qk[layer]
        scale = lax.rsqrt(head_mean(raw * raw) + EPS)
        normed = raw * scale
        low = (normed * qk_gain(layer)).astype(BF16)
        return low, normed, scale

    def probs_of(low, tile, half, mask):
        query = low[:, tile * 2 * HEAD : (tile + 1) * 2 * HEAD]
        key = low[:, 4 * HEAD :]
        query = jnp.where(halves[half], query, jnp.zeros_like(query))
        scores = dot(query, key, NT) * HEAD ** (-0.5)
        scores = jnp.where(mask, scores, NEG)
        expo = jnp.exp(scores - jnp.max(scores, axis=-1, keepdims=True))
        return expo / jnp.sum(expo, axis=-1, keepdims=True), query, key

    def weight_of(layer, half):
        return w_attn[layer, half].reshape(width, 6 * HEAD)

    def y_gather(row, buffer, layer):
        copies = [
            ring_copy(row, d, buffer.at[layer, shard], buffer.at[layer, shard], y_device(d))
            for d in (1, 3, 2)
        ]
        for copy in copies:
            copy.start()
        return copies

    def y_scatter(row):
        copies = [
            ring_copy(row, d, y_send.at[mod(shard + d)], y_recv.at[d - 1], y_device(d))
            for d in (1, 3, 2)
        ]
        for copy in copies:
            copy.start()
        return copies

    def y_total(copies):
        for copy in copies:
            copy.wait()
        total = y_send[shard].astype(F32)
        for d in (1, 2, 3):
            total = total + y_recv[d - 1].astype(F32)
        return total

    def spread_tokens(row, buffer, block):
        buffer[p] = block
        copies = [
            ring_copy(row, d, buffer.at[p], buffer.at[p], p_device(d)) for d in (1, 3, 2)
        ]
        for copy in copies:
            copy.start()
        return copies

    column_halves = (pl.ds(0, width // 2), pl.ds(width // 2, width // 2))

    def packed_copies(row, layer, f, target):
        return [
            ring_copy(
                row + f, d, packed_send.at[f, d - 1], target.at[layer, f, d], q_device(d)
            )
            for d in (1, 3, 2)
        ]

    def choose_all(layer, f):
        return jnp.concatenate(
            [choose_rows(layer, mod(q + d), f) for d in range(RING)], axis=0
        )

    def gates_all(layer, f):
        return jnp.concatenate(
            [
                jnp.broadcast_to(weights[layer, 2 * mod(q + d) + f], (group, span))
                for d in range(RING)
            ],
            axis=0,
        )

    def pack(row, layer, f, source, target, gated):
        chosen = choose_all(layer, f)
        low = chosen.astype(BF16)
        if gated:
            share = jnp.sum(
                jnp.where(chosen, gates_all(layer, f), 0.0), axis=1, keepdims=True
            )
        for cut in column_halves:
            block = dot(low, source[:, :, cut].reshape(span, width // 2))
            if gated:
                block = block * share
            block = block.astype(BF16)
            for d in (1, 3, 2):
                packed_send[f, d - 1, :, cut] = block[d * group : (d + 1) * group]
            target[layer, f, 0, :, cut] = block[:group]
        for copy in packed_copies(row, layer, f, target):
            copy.start()

    def result_copies(row, f, send, target):
        return [
            ring_copy(row + f, d, send.at[f, d - 1], target.at[f, d], q_device(-d))
            for d in (1, 3, 2)
        ]

    def put_result(row, f, send, target, columns):
        for cut in column_halves:
            block = columns(cut).astype(BF16)
            for d in (1, 3, 2):
                send[f, d - 1, :, cut] = block[d * group : (d + 1) * group]
            target[f, 0, :, cut] = block[:group]
        for copy in result_copies(row, f, send, target):
            copy.start()

    def combine(row, layer, send, target, gated):
        for f in range(2):
            chosen = choose_all(layer, f)
            if gated:
                share = jnp.where(chosen, gates_all(layer, f), 0.0)
            else:
                share = chosen.astype(F32)
            for copy in result_copies(row, f, send, target):
                copy.wait()
            share = share.astype(BF16)
            for cut in column_halves:
                total = dot(
                    share, target[f, :, :, cut].reshape(RING * group, width // 2), TN
                )
                if f == 0:
                    parts[:, cut] = total
                else:
                    total = total + parts[:, cut]
                    for i in range(RING):
                        partial_send[i, :, cut] = total[i * rows : (i + 1) * rows].astype(BF16)

    def partial_copies(row, target):
        return [
            ring_copy(
                row, d, partial_send.at[mod(p + d)], target.at[d - 1], p_device(d)
            )
            for d in (1, 3, 2)
        ]

    def start_partials(row, target):
        copies = partial_copies(row, target)
        for copy in copies:
            copy.start()
        return copies

    def total_of_partials(copies, target):
        for copy in copies:
            copy.wait()
        total = partial_send[p].astype(F32)
        for d in (1, 2, 3):
            total = total + target[d - 1].astype(F32)
        return total

    def wait_expert_weights(layer):
        @pl.when(core == layer)
        def _():
            for copy in local_weights():
                copy.wait()

        @pl.when(core != layer)
        def _():
            for copy in sent_weights():
                copy.wait_recv()

    def wait_all(copies):
        for copy in copies:
            copy.wait()

    def start_attention(layer):
        held = stream[layer]
        attn_all[layer, shard] = (held * scale_of(held) * gains[layer, 0:1, :]).astype(BF16)
        return y_gather(Y_GATHER, attn_all, layer)

    def attention(layer, copies):
        wait_all(copies)
        whole = attn_all[layer].reshape(span, width)
        raw_qk[layer] = dot(whole, weight_of(layer, 0))
        second_half = weight_of(layer, 1)
        values[layer] = dot(whole, second_half[:, : 2 * HEAD]).astype(BF16)
        low, _n, _s = normed_qk(layer)
        mask = allowed()
        value = values[layer]
        for tile in range(2):
            halves_out = []
            for half in range(2):
                probs, _q, _k = probs_of(low, tile, half, mask)
                halves_out.append(dot(probs.astype(BF16), value))
            mixed[layer, :, tile * 2 * HEAD : (tile + 1) * 2 * HEAD] = jnp.where(
                low_half, halves_out[0], halves_out[1]
            ).astype(BF16)
        out = dot(mixed[layer], second_half[:, 2 * HEAD :], NT)
        for i in range(RING):
            y_send[i] = out[i * rows : (i + 1) * rows].astype(BF16)
        return y_scatter(Y_SUM)

    def finish_attention(layer, copies):
        center = stream[layer] + y_total(copies)
        middle[layer] = center
        feed = (center * scale_of(center) * gains[layer, 1:2, :]).astype(BF16)
        return spread_tokens(TOKENS, tokens, feed)

    def feed_block(layer, f):
        return packed[layer, f].reshape(RING * group, width)

    def back_block(layer, f):
        return packed_back[layer, f].reshape(RING * group, width)

    def by_source(block):
        return block.astype(BF16).reshape(RING, group, hidden)

    def grad_core(kind):
        return core_copy(C_GRAD + kind, grads.at[other, kind], grads_core.at[kind])

    lower, upper = pl.ds(0, rows), pl.ds(rows, rows)

    def grad_ring(kind, step):
        ahead = step in (0, 2, 4)
        part, cut = (
            (2, lower),
            (2, upper),
            (1, upper),
            (-1, lower),
            (1, lower),
            (-1, upper),
        )[step]
        return pltpu.make_async_remote_copy(
            src_ref=grads.at[core, kind, mod(shard + part), cut],
            dst_ref=grads_y.at[kind, step],
            send_sem=g_send.at[kind, step],
            recv_sem=g_recv.at[kind, step],
            device_id=y_device(1 if ahead else -1),
            device_id_type=MESH,
        )

    def sum_cores():
        for kind in range(3):
            grad_core(kind).wait()

            def step(part, _):
                grads[core, kind, part] = (
                    grads[core, kind, part].astype(F32) + grads_core[kind, part].astype(F32)
                ).astype(BF16)
                return 0

            lax.fori_loop(0, RING, step, 0)
            for i in range(4):
                grad_ring(kind, i).start()

    def pass_grads():
        for kind in range(3):
            for i, part, cut in ((0, 1, lower), (1, -1, upper)):
                grad_ring(kind, i).wait()
                at = mod(shard + part)
                grads[core, kind, at, cut] = (
                    grads[core, kind, at, cut].astype(F32) + grads_y[kind, i].astype(F32)
                ).astype(BF16)
                grad_ring(kind, i + 4).start()

    def out_expert(layer):
        return core_copy(C_OUT_EXPERT + layer, out_stage, expert_out.at[:, core])

    def out_local():
        return pltpu.make_async_copy(out_stage, expert_out.at[:, core], out_sem)

    def finish_expert(layer):
        for kind in range(3):
            for i in (2, 3, 4, 5):
                grad_ring(kind, i).wait()
            for cut, merged, direct in ((lower, 4, 3), (upper, 5, 2)):
                out_stage[kind, cut] = (
                    grads[core, kind, shard, cut].astype(F32)
                    + grads_y[kind, merged].astype(F32)
                    + grads_y[kind, direct].astype(F32)
                )

        @pl.when(core == layer)
        def _():
            out_local().start()

        @pl.when(core != layer)
        def _():
            out_expert(layer).start()

    def wait_out(layer):
        @pl.when(core == layer)
        def _():
            out_local().wait()

        @pl.when(core != layer)
        def _():
            out_expert(layer).wait_send()

    def expert_grads(layer):
        for kind in range(3):
            def step(i, _):
                f, j = lax.div(i, 2), lax.rem(i, 2)
                cut = pl.ds(pl.multiple_of(j * 256, 256), 256)
                act = acts[kind, f, :, :, cut].reshape(RING * group, 256)
                rhs = back_block(layer, f) if kind == 2 else feed_block(layer, f)
                change = dot(act, rhs, TN).astype(BF16)
                grads[f, kind, 2 * j] = change[:128]
                grads[f, kind, 2 * j + 1] = change[128:]
                return 0

            lax.fori_loop(0, 4, step, 0)
            grad_core(kind).start()

    def proj_core_copy():
        return core_copy(C_PROJ, proj.at[other], proj_core)

    def proj_first(d, i):
        return pltpu.make_async_remote_copy(
            src_ref=proj.at[core, place_of(i, mod(p + d))],
            dst_ref=proj_recv.at[d - 1, i],
            send_sem=j_send.at[d - 1, i],
            recv_sem=j_recv.at[d - 1, i],
            device_id=p_device(d),
            device_id_type=MESH,
        )

    def proj_second(layer, d):
        return ring_copy(
            GRAD_Q + layer,
            d,
            proj_sum.at[mod(q + d)],
            proj_last.at[layer, d - 1],
            q_device(d),
        )

    def out_proj(layer):
        return core_copy(C_OUT_PROJ + layer, proj_stage, proj_out.at[core])

    def proj_one():
        proj_core_copy().wait()

        def step(i, _):
            proj[core, i] = (proj[core, i].astype(F32) + proj_core[i].astype(F32)).astype(BF16)
            return 0

        lax.fori_loop(0, RING * RING, step, 0)
        for i in range(RING):
            for d in (1, 3, 2):
                proj_first(d, i).start()

    def proj_two(layer):
        for i in range(RING):
            for d in (1, 3, 2):
                proj_first(d, i).wait()
            total = proj[core, place_of(i, p)].astype(F32)
            for d in (1, 2, 3):
                total = total + proj_recv[d - 1, i].astype(F32)
            proj_sum[i] = total.astype(BF16)
        for d in (1, 3, 2):
            proj_second(layer, d).start()

    def proj_three(layer):
        total = proj_sum[q].astype(F32)
        for d in (1, 3, 2):
            proj_second(layer, d).wait()
        for d in (1, 2, 3):
            total = total + proj_last[layer, d - 1].astype(F32)

        @pl.when(layer == core)
        def _():
            proj_out[core] = total

        @pl.when(layer != core)
        def _():
            proj_stage[...] = total
            out_proj(layer).start()

    def start_back(layer, incoming, change):
        center = middle[layer]
        scale = scale_of(center)
        normed = center * scale
        terms[layer, 1:2] = jnp.sum(change * normed, axis=0, keepdims=True)
        scaled = change * gains[layer, 1:2, :]
        inner = jnp.mean(scaled * normed, axis=-1, keepdims=True)
        back_mid = incoming + scale * (scaled - normed * inner)
        cotangent[...] = back_mid
        attn_back[layer, shard] = back_mid.astype(BF16)
        return y_gather(Y_GATHER_BACK, attn_back, layer)

    def attention_back(layer, copies):
        low, normed, scale = normed_qk(layer)
        wait_all(copies)
        whole_back = attn_back[layer].reshape(span, width)
        second_half = weight_of(layer, 1)
        back_mixed = dot(whole_back, second_half[:, 2 * HEAD :]).astype(BF16)
        value = values[layer]
        mask = allowed()
        back_key = jnp.zeros((span, 2 * HEAD), F32)
        back_value = jnp.zeros((span, 2 * HEAD), F32)
        tiles = []
        for tile in range(2):
            pieces = []
            for half in range(2):
                probs, query, key = probs_of(low, tile, half, mask)
                piece = back_mixed[:, tile * 2 * HEAD : (tile + 1) * 2 * HEAD]
                piece = jnp.where(halves[half], piece, jnp.zeros_like(piece))
                back_probs = dot(piece, value, NT)
                back_value = back_value + dot(probs.astype(BF16), piece, TN)
                total = jnp.sum(probs * back_probs, axis=-1, keepdims=True)
                back_scores = (probs * (back_probs - total)).astype(BF16)
                pieces.append(dot(back_scores, key))
                back_key = back_key + dot(back_scores, query, TN)
            tiles.append(jnp.where(low_half, pieces[0], pieces[1]))
        change = jnp.concatenate(tiles + [back_key], axis=1) * HEAD ** (-0.5)
        term = jnp.sum(change * normed, axis=0, keepdims=True)
        terms[layer, 2:3, : 6 * HEAD] = term
        scaled = change * qk_gain(layer)
        inner = head_mean(scaled * normed)
        back_qk[...] = (scale * (scaled - normed * inner)).astype(BF16)
        back_v[...] = back_value.astype(BF16)
        out = dot(back_qk[...], weight_of(layer, 0), NT) + dot(
            back_v[...], second_half[:, : 2 * HEAD], NT
        )
        for i in range(RING):
            y_send[i] = out[i * rows : (i + 1) * rows].astype(BF16)
        return y_scatter(Y_SUM_BACK)

    def proj_grads(layer):
        whole = attn_all[layer].reshape(span, width)
        whole_back = attn_back[layer].reshape(span, width)
        everyone = RING * RING
        first_part = dot(whole, back_qk[...], TN).astype(BF16)
        proj[0] = first_part.reshape(everyone, rows, 6 * HEAD)
        value_part = dot(whole, back_v[...], TN).astype(BF16)
        proj[1, :, :, : 2 * HEAD] = value_part.reshape(everyone, rows, 2 * HEAD)
        out_part = dot(whole_back, mixed[layer], TN).astype(BF16)
        proj[1, :, :, 2 * HEAD :] = out_part.reshape(everyone, rows, 4 * HEAD)
        proj_core_copy().start()

    def finish_back(layer, copies):
        total = y_total(copies)
        held = stream[layer]
        scale = scale_of(held)
        normed = held * scale
        terms[layer, 0:1] = jnp.sum(total * normed, axis=0, keepdims=True)
        scaled = total * gains[layer, 0:1, :]
        inner = jnp.mean(scaled * normed, axis=-1, keepdims=True)
        return (cotangent[...] + scale * (scaled - normed * inner)).astype(BF16)

    def slopes_of(gate_part, up_part):
        sigmoid = jax.nn.sigmoid(gate_part)
        silu = gate_part * sigmoid
        return up_part * sigmoid * (1.0 + gate_part * (1.0 - sigmoid)), silu

    def expert_back(layer, f, back_hidden, to_gate, to_up):
        back_gate = (back_hidden * to_gate).astype(BF16)
        back_up = (back_hidden * to_up).astype(BF16)
        acts[0, f] = by_source(back_gate)
        acts[1, f] = by_source(back_up)

        def columns(cut):
            return dot(back_gate, w_gate[layer, f, cut], NT) + dot(
                back_up, w_up[layer, f, cut], NT
            )

        put_result(RESULT_BACK, f, result_back_send, result_back, columns)

    def put_forward(layer, f, inner):
        def columns(cut):
            return dot(inner, w_down[layer, f, :, cut])

        put_result(RESULT, f, result_send, result, columns)

    terms[...] = jnp.zeros_like(terms)

    gather = start_attention(0)
    start_second(0)
    make_mask()
    make_tables()
    early = spread_tokens(TOKENS_BACK, tokens_back, cotangent[...].astype(BF16))
    start_half(0)
    for copy in sent_weights():
        copy.start()
    weight_half(0).wait_recv()
    scatter = attention(0, gather)
    start_second(1)
    take_tables()
    wait_all(early)
    for f in range(2):
        pack(PACKED_BACK, 1, f, tokens_back, packed_back, True)
    spread = finish_attention(0, scatter)
    start_half(1)
    for f in range(2):
        for copy in packed_copies(PACKED_BACK, 1, f, packed_back):
            copy.wait_send()
    wait_expert_weights(0)
    wait_all(spread)
    for f in range(2):
        pack(PACKED, 0, f, tokens, packed, False)
    for f in range(2):
        wait_all(packed_copies(PACKED, 0, f, packed))
        block = feed_block(0, f)
        gate_part = dot(block, w_gate[0, f])
        up_part = dot(block, w_up[0, f])
        inner = (gate_part * jax.nn.sigmoid(gate_part) * up_part).astype(BF16)
        put_forward(0, f, inner)
    combine(RESULT, 0, result_send, result, True)
    final = middle[0] + total_of_partials(start_partials(PARTIAL, partial), partial)
    stream[1] = final.astype(BF16).astype(F32)

    gather = start_attention(1)
    weight_half(1).wait_recv()
    scatter = attention(1, gather)
    for f in range(2):
        for copy in packed_copies(PACKED_BACK, 1, f, packed_back):
            copy.wait_recv()
    wait_expert_weights(1)
    spread = finish_attention(1, scatter)
    wait_all(spread)
    for f in range(2):
        pack(PACKED, 1, f, tokens, packed, False)
    for f in range(2):
        wait_all(packed_copies(PACKED, 1, f, packed))
        block = feed_block(1, f)
        gate_part = dot(block, w_gate[1, f])
        up_part = dot(block, w_up[1, f])
        back_hidden = dot(back_block(1, f), w_down[1, f], NT)
        to_gate, to_up = slopes_of(gate_part, up_part)
        acts[2, f] = by_source(to_up * up_part)
        expert_back(1, f, back_hidden, to_gate, to_up)
    for f in range(2):
        inner = acts[2, f].reshape(RING * group, hidden)
        put_forward(1, f, inner)
    expert_grads(1)
    combine(RESULT_BACK, 1, result_back_send, result_back, False)
    change = total_of_partials(start_partials(PARTIAL_BACK, partial_back), partial_back)

    gather = start_back(1, cotangent[...], change)
    combine(RESULT, 1, result_send, result, True)
    late = start_partials(PARTIAL, partial)
    sum_cores()
    pl.semaphore_signal(credit, inc=1, device_id=core_device, device_id_type=MESH)
    scatter = attention_back(1, gather)
    proj_grads(1)
    ends_stage[0] = (middle[1] + total_of_partials(late, partial)).astype(BF16)
    pass_grads()
    incoming = finish_back(1, scatter)
    cotangent[...] = incoming.astype(F32)

    spread = spread_tokens(TOKENS_BACK, tokens_back, incoming)
    proj_one()
    for f in range(2):
        block = feed_block(0, f)
        gate_part = dot(block, w_gate[0, f])
        up_part = dot(block, w_up[0, f])
        to_gate, to_up = slopes_of(gate_part, up_part)
        slopes[0, f] = to_gate
        slopes[1, f] = to_up
        acts[2, f] = by_source(to_up * up_part)
    wait_all(spread)
    for f in range(2):
        pack(PACKED_BACK, 0, f, tokens_back, packed_back, True)
    proj_two(1)
    for f in range(2):
        wait_all(packed_copies(PACKED_BACK, 0, f, packed_back))
        back_hidden = dot(back_block(0, f), w_down[0, f], NT)
        expert_back(0, f, back_hidden, slopes[0, f], slopes[1, f])
    finish_expert(1)
    for d in (1, -1):
        pl.semaphore_signal(y_credit, inc=1, device_id=y_device(d), device_id_type=MESH)
    pl.semaphore_wait(credit, 1)
    expert_grads(0)
    proj_three(1)
    combine(RESULT_BACK, 0, result_back_send, result_back, False)
    change = total_of_partials(start_partials(PARTIAL_BACK, partial_back), partial_back)
    gather = start_back(0, cotangent[...], change)
    pl.semaphore_wait(y_credit, 2)
    sum_cores()
    scatter = attention_back(0, gather)
    @pl.when(core != 1)
    def _():
        out_proj(1).wait_send()

    proj_grads(0)
    pass_grads()
    ends_stage[1] = finish_back(0, scatter)
    proj_one()

    ends_out[core] = jnp.where(first, ends_stage[1], ends_stage[0])
    ends_copy_out = core_copy(C_OUT_ENDS, ends_stage.at[core], ends_out.at[core])
    ends_copy_out.start()
    term_copy = core_copy(C_TERM, terms.at[other], terms_core)
    term_copy.start()
    term_copy.wait()
    terms_recv[0, 0] = terms[core] + terms_core[...]
    for axis, (row, device) in enumerate(
        ((GAIN_P, p_device), (GAIN_Q, q_device), (GAIN_Y, y_device))
    ):
        copies = [
            ring_copy(
                row, d, terms_recv.at[axis, 0], terms_recv.at[axis, d], device(d)
            )
            for d in (1, 3, 2)
        ]
        for copy in copies:
            copy.start()
        if axis == 0:
            proj_two(0)
        if axis == 1:
            proj_three(0)
        for copy in copies:
            copy.wait()
        total = terms_recv[axis, 0]
        for d in (1, 2, 3):
            total = total + terms_recv[axis, d]
        if axis < 2:
            terms_recv[axis + 1, 0] = total
        else:
            gains_out[...] = total

    wait_out(1)
    finish_expert(0)
    wait_out(0)
    for layer in range(2):
        @pl.when(core == layer)
        def _():
            out_expert(layer).wait_recv()
            out_proj(layer).wait_recv()

    @pl.when(core != 0)
    def _():
        out_proj(0).wait_send()

    ends_copy_out.wait()
    for copy in (piece_copy, ends_copy, gains_copy, routes_copy, gates_copy):
        copy.wait_send()
    for copy in sent_weights():
        copy.wait_send()
    for layer in range(2):
        weight_half(layer).wait_send()
        for d in (1, 2, 3):
            weight_first(layer, d).wait_send()
            for i in range(RING):
                weight_second(layer, d, i).wait_send()
    for d in (1, 2, 3):
        ring_copy(
            TABLE_P, d, table_send.at[d], table_recv.at[d - 1], p_device(d)
        ).wait_send()


def finish(
    ends_ref,
    gains_ref,
    proj_ref,
    experts_ref,
    ends_out,
    attn_gain_out,
    query_gain_out,
    key_gain_out,
    feed_gain_out,
    query_out,
    key_out,
    value_out,
    out_out,
    gate_out,
    up_out,
    down_out,
):
    ends_out[0] = ends_ref[...]
    attn_gain_out[...] = gains_ref[0:1]
    feed_gain_out[...] = gains_ref[1:2]
    query_gain_out[...] = exact_dot(gains_ref[2:3, : 4 * HEAD], copies_of_head(4), NT)
    key_gain_out[...] = exact_dot(gains_ref[2:3, 4 * HEAD : 6 * HEAD], copies_of_head(2), NT)
    swap = swap_heads()
    query_out[0] = exact_dot(proj_ref[0, :, : 4 * HEAD], swap)
    key_out[0] = proj_ref[0, :, 4 * HEAD :]
    value_out[0] = proj_ref[1, :, : 2 * HEAD]
    out_out[0] = exact_dot(proj_ref[1, :, 2 * HEAD :], swap)
    for f in range(2):
        gate_out[0, f] = experts_ref[0, f].T
        up_out[0, f] = experts_ref[1, f].T
        down_out[0, f] = experts_ref[2, f]


def shards(
    ends_in,
    segments,
    routes,
    gates,
    attn_gain,
    query_gain,
    key_gain,
    feed_gain,
    w_query,
    key_weight,
    value_weight,
    w_out,
    w_gate,
    w_up,
    w_down,
):
    rows = ends_in.shape[2]
    width = ends_in.shape[3]
    top = routes.shape[3]
    hidden = w_gate.shape[3]
    experts_all = w_gate.shape[1] * lax.axis_size("expert")
    capacity = 3 * rows * top // (2 * experts_all)
    group = RING * capacity
    span = RING * rows
    vmem = pl.BlockSpec(memory_space=pltpu.VMEM)
    anywhere = pl.BlockSpec(memory_space=pl.ANY)
    half = 6 * HEAD
    everyone = RING * RING
    scratch = [
        pltpu.VMEM((2, 2, width, hidden), BF16),
        pltpu.VMEM((2, 2, width, hidden), BF16),
        pltpu.VMEM((2, 2, hidden, width), BF16),
        pltpu.VMEM((2, 2, everyone, rows, half), BF16),
        pltpu.VMEM((rows, width), BF16),
        pltpu.VMEM((2, 8, width), F32),
        pltpu.VMEM((2, top, rows), jnp.int32),
        pltpu.VMEM((2, top, rows), F32),
        pltpu.VMEM((span, span), F32),
        pltpu.VMEM((2, rows, half), BF16),
        pltpu.VMEM((8, width), F32),
        pltpu.VMEM((RING, 2, 2, 8, span), F32),
        pltpu.VMEM((RING - 1, 2, 2, 8, span), F32),
        pltpu.VMEM((2, 8, 1, span), F32),
        pltpu.VMEM((2, 8, 1, span), F32),
        pltpu.VMEM((2, rows, width), F32),
        pltpu.VMEM((2, rows, width), F32),
        pltpu.VMEM((rows, width), F32),
        pltpu.VMEM((2, RING, rows, width), BF16),
        pltpu.VMEM((2, span, half), F32),
        pltpu.VMEM((2, span, 2 * HEAD), BF16),
        pltpu.VMEM((2, span, 4 * HEAD), BF16),
        pltpu.VMEM((RING, rows, width), BF16),
        pltpu.VMEM((RING - 1, rows, width), BF16),
        pltpu.VMEM((RING, rows, width), BF16),
        pltpu.VMEM((RING, rows, width), BF16),
        pltpu.VMEM((2, RING - 1, group, width), BF16),
        pltpu.VMEM((2, 2, RING, group, width), BF16),
        pltpu.VMEM((2, 2, RING, group, width), BF16),
        pltpu.VMEM((2, RING - 1, group, width), BF16),
        pltpu.VMEM((2, RING, group, width), BF16),
        pltpu.VMEM((2, RING - 1, group, width), BF16),
        pltpu.VMEM((2, RING, group, width), BF16),
        pltpu.VMEM((RING, rows, width), BF16),
        pltpu.VMEM((RING - 1, rows, width), BF16),
        pltpu.VMEM((RING - 1, rows, width), BF16),
        pltpu.VMEM((span, width), F32),
        pltpu.VMEM((2, 2, RING * group, hidden), F32),
        pltpu.VMEM((2, RING, rows, width), BF16),
        pltpu.VMEM((span, half), BF16),
        pltpu.VMEM((span, 2 * HEAD), BF16),
        pltpu.VMEM((3, 2, RING, group, hidden), BF16),
        pltpu.VMEM((2, 3, RING, hidden // RING, width), BF16),
        pltpu.VMEM((3, RING, hidden // RING, width), BF16),
        pltpu.VMEM((3, 6, rows, width), BF16),
        pltpu.VMEM((3, hidden // RING, width), F32),
        pltpu.VMEM((2, everyone, rows, half), BF16),
        pltpu.VMEM((everyone, rows, half), BF16),
        pltpu.VMEM((RING - 1, RING, rows, half), BF16),
        pltpu.VMEM((RING, rows, half), BF16),
        pltpu.VMEM((2, RING - 1, rows, half), BF16),
        pltpu.VMEM((rows, half), F32),
        pltpu.VMEM((2, 8, width), F32),
        pltpu.VMEM((8, width), F32),
        pltpu.VMEM((3, RING, 8, width), F32),
        pltpu.VMEM((2, rows, width), BF16),
        pltpu.SemaphoreType.DMA((RING_ROWS, RING - 1)),
        pltpu.SemaphoreType.DMA((RING_ROWS, RING - 1)),
        pltpu.SemaphoreType.DMA((2, RING - 1, RING)),
        pltpu.SemaphoreType.DMA((2, RING - 1, RING)),
        pltpu.SemaphoreType.DMA((RING - 1, RING)),
        pltpu.SemaphoreType.DMA((RING - 1, RING)),
        pltpu.SemaphoreType.DMA((3, 6)),
        pltpu.SemaphoreType.DMA((3, 6)),
        pltpu.SemaphoreType.DMA((CORE_ROWS,)),
        pltpu.SemaphoreType.DMA((CORE_ROWS,)),
        pltpu.SemaphoreType.DMA((3,)),
        pltpu.SemaphoreType.DMA,
        pltpu.SemaphoreType.REGULAR,
        pltpu.SemaphoreType.REGULAR,
    ]
    ends, gain_sums, proj, experts = pl.pallas_call(
        functools.partial(kernel, rows, width, hidden, capacity),
        out_shape=(
            jax.ShapeDtypeStruct((2, rows, width), BF16),
            jax.ShapeDtypeStruct((8, width), F32),
            jax.ShapeDtypeStruct((2, rows, half), F32),
            jax.ShapeDtypeStruct((3, 2, hidden // RING, width), F32),
        ),
        in_specs=[vmem] * 12 + [anywhere] * 3,
        out_specs=(vmem, vmem, vmem, anywhere),
        scratch_shapes=scratch,
        compiler_params=pltpu.CompilerParams(
            collective_id=0, has_side_effects=True, vmem_limit_bytes=62 << 20
        ),
        cost_estimate=pl.CostEstimate(
            flops=60_000_000_000, bytes_accessed=20_000_000, transcendentals=4_000_000
        ),
        name="layers",
    )(
        ends_in[0],
        segments,
        routes[0].transpose(0, 2, 1),
        gates[0].transpose(0, 2, 1),
        attn_gain,
        query_gain,
        key_gain,
        feed_gain,
        w_query[0],
        key_weight[0],
        value_weight[0],
        w_out[0].T,
        w_gate[0],
        w_up[0],
        w_down[0],
    )
    shapes = (
        ((1, 2, rows, width), BF16),
        ((1, width), F32),
        ((1, HEAD), F32),
        ((1, HEAD), F32),
        ((1, width), F32),
        ((1,) + w_query.shape[1:], F32),
        ((1,) + key_weight.shape[1:], F32),
        ((1,) + value_weight.shape[1:], F32),
        ((1, w_out.shape[2], w_out.shape[1]), F32),
        ((1, 2, width, hidden // RING), F32),
        ((1, 2, width, hidden // RING), F32),
        ((1, 2, hidden // RING, width), F32),
    )
    outputs = pl.pallas_call(
        finish,
        out_shape=tuple(jax.ShapeDtypeStruct(shape, dtype) for shape, dtype in shapes),
        in_specs=[vmem] * 4,
        out_specs=(vmem,) * len(shapes),
        compiler_params=pltpu.CompilerParams(vmem_limit_bytes=32 << 20),
        name="finish",
    )(ends, gain_sums, proj, experts)
    return (*outputs[:8], outputs[8].transpose(0, 2, 1), *outputs[9:])


def solution(mesh):
    return jax.shard_map(
        shards,
        mesh=mesh,
        in_specs=(
            P("section", None, ("expert", "shard"), None),
            P(None, "expert"),
            P("section", None, ("expert", "shard"), None),
            P("section", None, ("expert", "shard"), None),
            P("section", None),
            P("section", None),
            P("section", None),
            P("section", None),
            P("section", "expert", "shard"),
            P("section", "expert", "shard"),
            P("section", "expert", "shard"),
            P("section", "shard", "expert"),
            P("section", "expert", None, None),
            P("section", "expert", None, None),
            P("section", "expert", None, None),
        ),
        out_specs=(
            P("section", None, ("expert", "shard"), None),
            P("section", None),
            P("section", None),
            P("section", None),
            P("section", None),
            P("section", "expert", "shard"),
            P("section", "expert", "shard"),
            P("section", "expert", "shard"),
            P("section", "shard", "expert"),
            P("section", "expert", None, "shard"),
            P("section", "expert", None, "shard"),
            P("section", "expert", "shard", None),
        ),
        check_vma=False,
    )
```

profile of v0, /device:TPU:0, one launch (start us, length us, event | category | flops | bytes accessed | tf_op | source)
XLA Modules:
  0.0 255.5 jit_solution(10509447311185858858)
XLA Ops:
  0.7 248.0 %layers.1 = (bf16[2,64,1024]{2,1,0:T(8,128)(2,1)}, f32[8,1024]{1,0:T(8,128)}, f32[2,64,384]{2,1,0:T(8,128)}, f32[3,2,128,1024]{3,2,1,0:T(8,128)}) custom-call(bf16[2,64,1024]{2,1,0:T(8,128)(2,1)} %bitcast.20, s32[2,256]{1,0:T(2,128)} %segments_ref.1, s32[2,8,64]{2,1,0:T(8,128)} %bitcast.26, f32[2,8,64]{2,1,0:T(8,128)} %bitcast.27, f32[1,1024]{1,0:T(1,128)} %attn_gain_ref.1, ...), custom_call_target="tpu_custom_call" | custom-call | flops 60000002048 | bytes 20000000 | tf_op jit(solution)/shard_map/layers/pallas_call | solution.py:1199
  248.7 0.0 copy-start
  248.7 1.9 copy-done
  250.6 0.0 copy-start.1
  250.6 0.9 copy-done.1
  251.5 0.0 copy-start.2
  251.5 0.9 copy-done.2
  252.4 0.0 copy-start.3
  252.4 0.8 copy-done.3
  253.2 2.3 finish.1
Async XLA Ops:
  248.7 1.9 copy-start
  250.6 0.9 copy-start.1
  251.5 0.9 copy-start.2
  252.4 0.8 copy-start.3
where the time goes:
time: 256 us; the launch traced here: 255 us
  Pallas kernels  250 us (98%)
  local copies, waits for them, and re-layouts  4.52 us (2%)
    pallas_call x1, Pallas kernels, shards(): pl.pallas_call(functools.partial(kernel, rows, width, hidden, capacity),...  248 us

commit v1 on v0

--- a/solution.py
+++ b/solution.py
@@ -19,57 +19,14 @@
 NT = (((1,), (1,)), ((), ()))
 TN = (((0,), (0,)), ((), ()))
 
-(
-    Y_GATHER,
-    Y_SUM,
-    Y_GATHER_BACK,
-    Y_SUM_BACK,
-    TOKENS,
-    TOKENS_BACK,
-    PACKED,
-    _packed_next,
-    PACKED_BACK,
-    _packed_back_next,
-    RESULT,
-    _result_next,
-    RESULT_BACK,
-    _result_back_next,
-    PARTIAL,
-    PARTIAL_BACK,
-    GRAD_Q,
-    _grad_q_next,
-    GAIN_P,
-    GAIN_Q,
-    GAIN_Y,
-    WEIGHT_P,
-    _weight_p_next,
-    TABLE_P,
-    RING_ROWS,
-) = range(25)
-
-(
-    C_ENDS,
-    C_GAINS,
-    C_ROUTES,
-    C_GATES,
-    C_PIECE,
-    C_HALF,
-    _half_next,
-    C_GATE,
-    C_UP,
-    C_DOWN,
-    C_GRAD,
-    _grad_next,
-    _grad_last,
-    C_PROJ,
-    C_TERM,
-    C_OUT_EXPERT,
-    _out_expert_next,
-    C_OUT_PROJ,
-    _out_proj_next,
-    C_OUT_ENDS,
-    CORE_ROWS,
-) = range(21)
+Y_GATHER, Y_SUM, Y_GATHER_BACK, Y_SUM_BACK, TOKENS, TOKENS_BACK = range(6)
+PARTIAL, PARTIAL_BACK, GRAD_Q, GAIN_P, GAIN_Q, GAIN_Y = 6, 7, 8, 10, 11, 12
+WEIGHT_P, TABLE_P = 13, 15
+PACKED, PACKED_BACK, RESULT, RESULT_BACK, RING_ROWS = 16, 20, 24, 28, 32
+
+C_ENDS, C_GAINS, C_ROUTES, C_GATES, C_PIECE = range(5)
+C_GATE, C_UP, C_DOWN, C_GRAD, C_PROJ, C_TERM, C_OUT_ENDS = 5, 6, 7, 8, 11, 12, 13
+C_OUT_EXPERT, C_OUT_PROJ, CORE_ROWS = 14, 20, 22
 
 
 def dot(a, b, form=NN):
@@ -158,7 +115,6 @@
     packed_back,
     result_send,
     result,
-    result_back_send,
     result_back,
     partial_send,
     partial,
@@ -187,6 +143,8 @@
     recv_sem,
     w_send,
     w_recv,
+    h_send,
+    h_recv,
     j_send,
     j_recv,
     g_send,
@@ -207,6 +165,8 @@
     q = z + core * (x - z)
     span = RING * rows
     group = RING * capacity
+    part_rows = group // 2
+    chunk = RING * part_rows
     other = 1 - core
 
     def mod(value):
@@ -251,7 +211,13 @@
         for device in (y_device(d), p_device(d), q_device(d)):
             pl.semaphore_signal(barrier, inc=1, device_id=device, device_id_type=MESH)
     pl.semaphore_signal(barrier, inc=1, device_id=core_device, device_id_type=MESH)
-    pl.semaphore_wait(barrier, 10)
+
+    def local_weights():
+        return (
+            pltpu.make_async_copy(gate_ref, w_gate.at[core], local_sem.at[0]),
+            pltpu.make_async_copy(up_ref, w_up.at[core], local_sem.at[1]),
+            pltpu.make_async_copy(down_ref, w_down.at[core], local_sem.at[2]),
+        )
 
     swap = swap_heads().astype(BF16)
     piece_ref[0, :, : 4 * HEAD] = dot(query_ref[...], swap).astype(BF16)
@@ -262,6 +228,20 @@
     gains_ref[1:2] = feed_gain_ref[...]
     gains_ref[2:3, : 4 * HEAD] = exact_dot(query_gain_ref[...], copies_of_head(4))
     gains_ref[2:3, 4 * HEAD : 6 * HEAD] = exact_dot(key_gain_ref[...], copies_of_head(2))
+    w_attn[core, core, place] = piece_ref[core]
+    gains[core] = gains_ref[...]
+    routes[core] = routes_ref[core]
+    gates[core] = gates_ref[core]
+    across = jnp.broadcast_to(
+        jnp.where(core == 0, segments_ref[0:1], segments_ref[1:2]), (span, span)
+    ).astype(F32)
+    causal = iota((span, span), 0) >= iota((span, span), 1)
+    mask_ref[...] = (causal & (across == across.T)).astype(F32)
+    terms[...] = jnp.zeros_like(terms)
+    for copy in local_weights():
+        copy.start()
+
+    pl.semaphore_wait(barrier, 10)
     piece_copy = core_copy(C_PIECE, piece_ref.at[other], w_attn.at[core, other, place])
     ends_copy = core_copy(C_ENDS, ends_ref.at[other], ends_in)
     gains_copy = core_copy(C_GAINS, gains_ref, gains.at[core])
@@ -269,17 +249,6 @@
     gates_copy = core_copy(C_GATES, gates_ref.at[other], gates.at[core])
     for copy in (piece_copy, ends_copy, gains_copy, routes_copy, gates_copy):
         copy.start()
-    w_attn[core, core, place] = piece_ref[core]
-    gains[core] = gains_ref[...]
-    routes[core] = routes_ref[core]
-    gates[core] = gates_ref[core]
-
-    def local_weights():
-        return (
-            pltpu.make_async_copy(gate_ref, w_gate.at[core], local_sem.at[0]),
-            pltpu.make_async_copy(up_ref, w_up.at[core], local_sem.at[1]),
-            pltpu.make_async_copy(down_ref, w_down.at[core], local_sem.at[2]),
-        )
 
     def sent_weights():
         return (
@@ -287,9 +256,6 @@
             core_copy(C_UP, up_ref, w_up.at[core]),
             core_copy(C_DOWN, down_ref, w_down.at[core]),
         )
-
-    for copy in local_weights():
-        copy.start()
 
     def weight_first(layer, d):
         return pltpu.make_async_remote_copy(
@@ -312,8 +278,16 @@
             device_id_type=MESH,
         )
 
-    def weight_half(layer):
-        return core_copy(C_HALF + layer, w_attn.at[layer, core], w_attn.at[layer, core])
+    def weight_pass(layer, d, i):
+        held = place_of(mod(q - d), mod(p - i))
+        return pltpu.make_async_remote_copy(
+            src_ref=w_attn.at[layer, core, held],
+            dst_ref=w_attn.at[layer, core, held],
+            send_sem=h_send.at[layer, d, i],
+            recv_sem=h_recv.at[layer, d, i],
+            device_id=core_device,
+            device_id_type=MESH,
+        )
 
     def start_first(layer):
         for d in (1, 3, 2):
@@ -325,12 +299,18 @@
                 weight_first(layer, i).wait_recv()
             for d in (1, 3, 2):
                 weight_second(layer, d, i).start()
-
-    def start_half(layer):
+            weight_pass(layer, 0, i).start()
+
+    def start_pass(layer):
         for i in (0, 1, 3, 2):
             for d in (1, 3, 2):
                 weight_second(layer, d, i).wait_recv()
-        weight_half(layer).start()
+                weight_pass(layer, d, i).start()
+
+    def wait_pass(layer):
+        for d in range(RING):
+            for i in range(RING):
+                weight_pass(layer, d, i).wait_recv()
 
     piece_copy.wait_recv()
     start_first(0)
@@ -385,9 +365,9 @@
                 for r in range(2 * RING):
                     target[layer, r] = whole[r : r + 1, :]
 
-    def choose_rows(layer, second, f):
-        at = lax.broadcasted_iota(jnp.int32, (group, span), 0).astype(F32) + 1.0
-        return at == slots[layer, 2 * second + f]
+    def choose_rows(layer, second, f, h):
+        at = iota((part_rows, span), 0) + (1 + part_rows * h)
+        return at.astype(F32) == slots[layer, 2 * second + f]
 
     lanes = lax.broadcasted_iota(jnp.int32, (1, 2 * HEAD), 1)
     low_half = lanes < HEAD
@@ -406,13 +386,6 @@
     def qk_gain(layer):
         return gains[layer, 2:3, : 6 * HEAD]
 
-    def make_mask():
-        across = jnp.broadcast_to(
-            jnp.where(core == 0, segments_ref[0:1], segments_ref[1:2]), (span, span)
-        ).astype(F32)
-        causal = iota((span, span), 0) >= iota((span, span), 1)
-        mask_ref[...] = (causal & (across == across.T)).astype(F32)
-
     def allowed():
         return mask_ref[...] != 0.0
 
@@ -432,8 +405,11 @@
         expo = jnp.exp(scores - jnp.max(scores, axis=-1, keepdims=True))
         return expo / jnp.sum(expo, axis=-1, keepdims=True), query, key
 
-    def weight_of(layer, half):
-        return w_attn[layer, half].reshape(width, 6 * HEAD)
+    half_rows = (slice(0, 8), slice(8, 16))
+
+    def weight_of(layer, half, start, stop, places=slice(0, 16)):
+        block = w_attn[layer, half, places, :, start * HEAD : stop * HEAD]
+        return block.reshape(block.shape[0] * rows, (stop - start) * HEAD)
 
     def y_gather(row, buffer, layer):
         copies = [
@@ -472,81 +448,102 @@
 
     column_halves = (pl.ds(0, width // 2), pl.ds(width // 2, width // 2))
 
-    def packed_copies(row, layer, f, target):
+    def packed_copies(row, layer, f, h, target):
         return [
             ring_copy(
-                row + f, d, packed_send.at[f, d - 1], target.at[layer, f, d], q_device(d)
+                row + 2 * f + h,
+                d,
+                packed_send.at[f, h, d - 1],
+                target.at[layer, f, h, d],
+                q_device(d),
             )
             for d in (1, 3, 2)
         ]
 
-    def choose_all(layer, f):
+    def choose_all(layer, f, h):
         return jnp.concatenate(
-            [choose_rows(layer, mod(q + d), f) for d in range(RING)], axis=0
+            [choose_rows(layer, mod(q + d), f, h) for d in range(RING)], axis=0
         )
 
     def gates_all(layer, f):
         return jnp.concatenate(
             [
-                jnp.broadcast_to(weights[layer, 2 * mod(q + d) + f], (group, span))
+                jnp.broadcast_to(weights[layer, 2 * mod(q + d) + f], (part_rows, span))
                 for d in range(RING)
             ],
             axis=0,
         )
 
-    def pack(row, layer, f, source, target, gated):
-        chosen = choose_all(layer, f)
-        low = chosen.astype(BF16)
-        if gated:
-            share = jnp.sum(
-                jnp.where(chosen, gates_all(layer, f), 0.0), axis=1, keepdims=True
+    def each_chunk(step):
+        def body(i, _):
+            step(lax.div(i, 2), lax.rem(i, 2))
+            return 0
+
+        lax.fori_loop(0, 4, body, 0)
+
+    def pack(row, layer, source, target, gated):
+        def step(f, h):
+            chosen = choose_all(layer, f, h)
+            low = chosen.astype(BF16)
+            if gated:
+                share = jnp.sum(
+                    jnp.where(chosen, gates_all(layer, f), 0.0), axis=1, keepdims=True
+                )
+            for cut in column_halves:
+                block = dot(low, source[:, :, cut].reshape(span, width // 2))
+                if gated:
+                    block = block * share
+                block = block.astype(BF16)
+                for d in (1, 3, 2):
+                    packed_send[f, h, d - 1, :, cut] = block[
+                        d * part_rows : (d + 1) * part_rows
+                    ]
+                target[layer, f, h, 0, :, cut] = block[:part_rows]
+            for copy in packed_copies(row, layer, f, h, target):
+                copy.start()
+
+        each_chunk(step)
+
+    def result_copies(row, f, h, send, target):
+        return [
+            ring_copy(
+                row + 2 * f + h,
+                d,
+                send.at[f, h, d - 1],
+                target.at[f, h, d],
+                q_device(-d),
             )
-        for cut in column_halves:
-            block = dot(low, source[:, :, cut].reshape(span, width // 2))
-            if gated:
-                block = block * share
-            block = block.astype(BF16)
-            for d in (1, 3, 2):
-                packed_send[f, d - 1, :, cut] = block[d * group : (d + 1) * group]
-            target[layer, f, 0, :, cut] = block[:group]
-        for copy in packed_copies(row, layer, f, target):
-            copy.start()
-
-    def result_copies(row, f, send, target):
-        return [
-            ring_copy(row + f, d, send.at[f, d - 1], target.at[f, d], q_device(-d))
             for d in (1, 3, 2)
         ]
 
-    def put_result(row, f, send, target, columns):
+    def put_result(row, f, h, send, target, columns):
         for cut in column_halves:
             block = columns(cut).astype(BF16)
             for d in (1, 3, 2):
-                send[f, d - 1, :, cut] = block[d * group : (d + 1) * group]
-            target[f, 0, :, cut] = block[:group]
-        for copy in result_copies(row, f, send, target):
+                send[f, h, d - 1, :, cut] = block[d * part_rows : (d + 1) * part_rows]
+            target[f, h, 0, :, cut] = block[:part_rows]
+        for copy in result_copies(row, f, h, send, target):
             copy.start()
 
     def combine(row, layer, send, target, gated):
-        for f in range(2):
-            chosen = choose_all(layer, f)
+        parts[...] = jnp.zeros_like(parts)
+
+        def step(f, h):
+            chosen = choose_all(layer, f, h)
             if gated:
                 share = jnp.where(chosen, gates_all(layer, f), 0.0)
             else:
                 share = chosen.astype(F32)
-            for copy in result_copies(row, f, send, target):
-                copy.wait()
             share = share.astype(BF16)
+            wait_all(result_copies(row, f, h, send, target))
             for cut in column_halves:
-                total = dot(
-                    share, target[f, :, :, cut].reshape(RING * group, width // 2), TN
+                parts[:, cut] += dot(
+                    share, target[f, h, :, :, cut].reshape(chunk, width // 2), TN
                 )
-                if f == 0:
-                    parts[:, cut] = total
-                else:
-                    total = total + parts[:, cut]
-                    for i in range(RING):
-                        partial_send[i, :, cut] = total[i * rows : (i + 1) * rows].astype(BF16)
+
+        each_chunk(step)
+        for i in range(RING):
+            partial_send[i] = parts[i * rows : (i + 1) * rows].astype(BF16)
 
     def partial_copies(row, target):
         return [
@@ -593,9 +590,8 @@
     def attention(layer, copies):
         wait_all(copies)
         whole = attn_all[layer].reshape(span, width)
-        raw_qk[layer] = dot(whole, weight_of(layer, 0))
-        second_half = weight_of(layer, 1)
-        values[layer] = dot(whole, second_half[:, : 2 * HEAD]).astype(BF16)
+        raw_qk[layer] = dot(whole, weight_of(layer, 0, 0, 6))
+        values[layer] = dot(whole, weight_of(layer, 1, 0, 2)).astype(BF16)
         low, _n, _s = normed_qk(layer)
         mask = allowed()
         value = values[layer]
@@ -607,9 +603,10 @@
             mixed[layer, :, tile * 2 * HEAD : (tile + 1) * 2 * HEAD] = jnp.where(
                 low_half, halves_out[0], halves_out[1]
             ).astype(BF16)
-        out = dot(mixed[layer], second_half[:, 2 * HEAD :], NT)
-        for i in range(RING):
-            y_send[i] = out[i * rows : (i + 1) * rows].astype(BF16)
+        for places, cut in zip(half_rows, column_halves):
+            out = dot(mixed[layer], weight_of(layer, 1, 2, 6, places), NT)
+            for i in range(RING):
+                y_send[i, :, cut] = out[i * rows : (i + 1) * rows].astype(BF16)
         return y_scatter(Y_SUM)
 
     def finish_attention(layer, copies):
@@ -624,8 +621,11 @@
     def back_block(layer, f):
         return packed_back[layer, f].reshape(RING * group, width)
 
-    def by_source(block):
-        return block.astype(BF16).reshape(RING, group, hidden)
+    def feed_chunk(layer, f, h):
+        return packed[layer, f, h].reshape(chunk, width)
+
+    def back_chunk(layer, f, h):
+        return packed_back[layer, f, h].reshape(chunk, width)
 
     def grad_core(kind):
         return core_copy(C_GRAD + kind, grads.at[other, kind], grads_core.at[kind])
@@ -651,70 +651,74 @@
             device_id_type=MESH,
         )
 
-    def sum_cores():
-        for kind in range(3):
-            grad_core(kind).wait()
-
-            def step(part, _):
-                grads[core, kind, part] = (
-                    grads[core, kind, part].astype(F32) + grads_core[kind, part].astype(F32)
-                ).astype(BF16)
-                return 0
-
-            lax.fori_loop(0, RING, step, 0)
-            for i in range(4):
-                grad_ring(kind, i).start()
-
-    def pass_grads():
-        for kind in range(3):
-            for i, part, cut in ((0, 1, lower), (1, -1, upper)):
-                grad_ring(kind, i).wait()
-                at = mod(shard + part)
-                grads[core, kind, at, cut] = (
-                    grads[core, kind, at, cut].astype(F32) + grads_y[kind, i].astype(F32)
-                ).astype(BF16)
-                grad_ring(kind, i + 4).start()
-
-    def out_expert(layer):
-        return core_copy(C_OUT_EXPERT + layer, out_stage, expert_out.at[:, core])
-
-    def out_local():
-        return pltpu.make_async_copy(out_stage, expert_out.at[:, core], out_sem)
-
-    def finish_expert(layer):
-        for kind in range(3):
-            for i in (2, 3, 4, 5):
-                grad_ring(kind, i).wait()
-            for cut, merged, direct in ((lower, 4, 3), (upper, 5, 2)):
-                out_stage[kind, cut] = (
-                    grads[core, kind, shard, cut].astype(F32)
-                    + grads_y[kind, merged].astype(F32)
-                    + grads_y[kind, direct].astype(F32)
-                )
+    def sum_cores(kind):
+        grad_core(kind).wait()
+
+        def step(part, _):
+            grads[core, kind, part] = (
+                grads[core, kind, part].astype(F32) + grads_core[kind, part].astype(F32)
+            ).astype(BF16)
+            return 0
+
+        lax.fori_loop(0, RING, step, 0)
+
+    def start_ring(kind):
+        for i in range(4):
+            grad_ring(kind, i).start()
+
+    def pass_grads(kind):
+        for i, part, cut in ((0, 1, lower), (1, -1, upper)):
+            grad_ring(kind, i).wait()
+            at = mod(shard + part)
+            grads[core, kind, at, cut] = (
+                grads[core, kind, at, cut].astype(F32) + grads_y[kind, i].astype(F32)
+            ).astype(BF16)
+            grad_ring(kind, i + 4).start()
+
+    def out_expert(layer, kind):
+        return core_copy(
+            C_OUT_EXPERT + 3 * layer + kind, out_stage.at[kind], expert_out.at[kind, core]
+        )
+
+    def out_local(kind):
+        return pltpu.make_async_copy(
+            out_stage.at[kind], expert_out.at[kind, core], out_sem.at[kind]
+        )
+
+    def finish_expert(layer, kind):
+        for i in (2, 3, 4, 5):
+            grad_ring(kind, i).wait()
+        for cut, merged, direct in ((lower, 4, 3), (upper, 5, 2)):
+            out_stage[kind, cut] = (
+                grads[core, kind, shard, cut].astype(F32)
+                + grads_y[kind, merged].astype(F32)
+                + grads_y[kind, direct].astype(F32)
+            )
 
         @pl.when(core == layer)
         def _():
-            out_local().start()
+            out_local(kind).start()
 
         @pl.when(core != layer)
         def _():
-            out_expert(layer).start()
+            out_expert(layer, kind).start()
 
     def wait_out(layer):
-        @pl.when(core == layer)
-        def _():
-            out_local().wait()
-
-        @pl.when(core != layer)
-        def _():
-            out_expert(layer).wait_send()
+        for kind in range(3):
+            @pl.when(core == layer)
+            def _():
+                out_local(kind).wait()
+
+            @pl.when(core != layer)
+            def _():
+                out_expert(layer, kind).wait_send()
 
     def expert_grads(layer):
         for kind in range(3):
             def step(i, _):
                 f, j = lax.div(i, 2), lax.rem(i, 2)
                 cut = pl.ds(pl.multiple_of(j * 256, 256), 256)
-                act = acts[kind, f, :, :, cut].reshape(RING * group, 256)
+                act = acts[kind, f, :, :, cut].reshape(2 * chunk, 256)
                 rhs = back_block(layer, f) if kind == 2 else feed_block(layer, f)
                 change = dot(act, rhs, TN).astype(BF16)
                 grads[f, kind, 2 * j] = change[:128]
@@ -800,12 +804,10 @@
         attn_back[layer, shard] = back_mid.astype(BF16)
         return y_gather(Y_GATHER_BACK, attn_back, layer)
 
-    def attention_back(layer, copies):
+    def attention_back(layer):
         low, normed, scale = normed_qk(layer)
-        wait_all(copies)
         whole_back = attn_back[layer].reshape(span, width)
-        second_half = weight_of(layer, 1)
-        back_mixed = dot(whole_back, second_half[:, 2 * HEAD :]).astype(BF16)
+        back_mixed = dot(whole_back, weight_of(layer, 1, 2, 6)).astype(BF16)
         value = values[layer]
         mask = allowed()
         back_key = jnp.zeros((span, 2 * HEAD), F32)
@@ -831,23 +833,31 @@
         inner = head_mean(scaled * normed)
         back_qk[...] = (scale * (scaled - normed * inner)).astype(BF16)
         back_v[...] = back_value.astype(BF16)
-        out = dot(back_qk[...], weight_of(layer, 0), NT) + dot(
-            back_v[...], second_half[:, : 2 * HEAD], NT
-        )
-        for i in range(RING):
-            y_send[i] = out[i * rows : (i + 1) * rows].astype(BF16)
+        for places, cut in zip(half_rows, column_halves):
+            out = dot(back_qk[...], weight_of(layer, 0, 0, 6, places), NT)
+            out = out + dot(back_v[...], weight_of(layer, 1, 0, 2, places), NT)
+            for i in range(RING):
+                y_send[i, :, cut] = out[i * rows : (i + 1) * rows].astype(BF16)
         return y_scatter(Y_SUM_BACK)
 
     def proj_grads(layer):
-        whole = attn_all[layer].reshape(span, width)
-        whole_back = attn_back[layer].reshape(span, width)
-        everyone = RING * RING
-        first_part = dot(whole, back_qk[...], TN).astype(BF16)
-        proj[0] = first_part.reshape(everyone, rows, 6 * HEAD)
-        value_part = dot(whole, back_v[...], TN).astype(BF16)
-        proj[1, :, :, : 2 * HEAD] = value_part.reshape(everyone, rows, 2 * HEAD)
-        out_part = dot(whole_back, mixed[layer], TN).astype(BF16)
-        proj[1, :, :, 2 * HEAD :] = out_part.reshape(everyone, rows, 4 * HEAD)
+        def step(i, _):
+            cut = pl.ds(pl.multiple_of(i * 4 * rows, 4 * rows), 4 * rows)
+            at = pl.ds(i * 4, 4)
+            feed = attn_all[layer, :, :, cut].reshape(span, 4 * rows)
+            back = attn_back[layer, :, :, cut].reshape(span, 4 * rows)
+            for half, start, stop, lhs, rhs in (
+                (0, 0, 6, feed, back_qk[...]),
+                (1, 0, 2, feed, back_v[...]),
+                (1, 2, 6, back, mixed[layer]),
+            ):
+                change = dot(lhs, rhs, TN).astype(BF16)
+                proj[half, at, :, start * HEAD : stop * HEAD] = change.reshape(
+                    4, rows, (stop - start) * HEAD
+                )
+            return 0
+
+        lax.fori_loop(0, 4, step, 0)
         proj_core_copy().start()
 
     def finish_back(layer, copies):
@@ -865,145 +875,171 @@
         silu = gate_part * sigmoid
         return up_part * sigmoid * (1.0 + gate_part * (1.0 - sigmoid)), silu
 
-    def expert_back(layer, f, back_hidden, to_gate, to_up):
+    def expert_back(layer, f, h, back_hidden, to_gate, to_up):
         back_gate = (back_hidden * to_gate).astype(BF16)
         back_up = (back_hidden * to_up).astype(BF16)
-        acts[0, f] = by_source(back_gate)
-        acts[1, f] = by_source(back_up)
+        acts[0, f, h] = back_gate
+        acts[1, f, h] = back_up
 
         def columns(cut):
             return dot(back_gate, w_gate[layer, f, cut], NT) + dot(
                 back_up, w_up[layer, f, cut], NT
             )
 
-        put_result(RESULT_BACK, f, result_back_send, result_back, columns)
-
-    def put_forward(layer, f, inner):
+        put_result(RESULT_BACK, f, h, packed_send, result_back, columns)
+
+    def put_forward(layer, f, h, inner):
         def columns(cut):
             return dot(inner, w_down[layer, f, :, cut])
 
-        put_result(RESULT, f, result_send, result, columns)
-
-    terms[...] = jnp.zeros_like(terms)
+        put_result(RESULT, f, h, result_send, result, columns)
+
+    def gate_and_up(layer, f, h):
+        block = feed_chunk(layer, f, h)
+        return dot(block, w_gate[layer, f]), dot(block, w_up[layer, f])
 
     gather = start_attention(0)
     start_second(0)
-    make_mask()
     make_tables()
     early = spread_tokens(TOKENS_BACK, tokens_back, cotangent[...].astype(BF16))
-    start_half(0)
+    start_pass(0)
     for copy in sent_weights():
         copy.start()
-    weight_half(0).wait_recv()
+    wait_pass(0)
     scatter = attention(0, gather)
     start_second(1)
     take_tables()
     wait_all(early)
-    for f in range(2):
-        pack(PACKED_BACK, 1, f, tokens_back, packed_back, True)
+    pack(PACKED_BACK, 1, tokens_back, packed_back, True)
     spread = finish_attention(0, scatter)
-    start_half(1)
-    for f in range(2):
-        for copy in packed_copies(PACKED_BACK, 1, f, packed_back):
+    start_pass(1)
+
+    def packed_back_sent(f, h):
+        for copy in packed_copies(PACKED_BACK, 1, f, h, packed_back):
             copy.wait_send()
+
+    each_chunk(packed_back_sent)
     wait_expert_weights(0)
     wait_all(spread)
-    for f in range(2):
-        pack(PACKED, 0, f, tokens, packed, False)
-    for f in range(2):
-        wait_all(packed_copies(PACKED, 0, f, packed))
-        block = feed_block(0, f)
-        gate_part = dot(block, w_gate[0, f])
-        up_part = dot(block, w_up[0, f])
+    pack(PACKED, 0, tokens, packed, False)
+
+    def experts_forward(f, h):
+        wait_all(packed_copies(PACKED, 0, f, h, packed))
+        gate_part, up_part = gate_and_up(0, f, h)
         inner = (gate_part * jax.nn.sigmoid(gate_part) * up_part).astype(BF16)
-        put_forward(0, f, inner)
+        put_forward(0, f, h, inner)
+
+    each_chunk(experts_forward)
     combine(RESULT, 0, result_send, result, True)
     final = middle[0] + total_of_partials(start_partials(PARTIAL, partial), partial)
     stream[1] = final.astype(BF16).astype(F32)
 
     gather = start_attention(1)
-    weight_half(1).wait_recv()
+    wait_pass(1)
+    wait_expert_weights(1)
+
+    def hidden_back(f, h):
+        for copy in packed_copies(PACKED_BACK, 1, f, h, packed_back):
+            copy.wait_recv()
+        slopes[0, f, h] = dot(back_chunk(1, f, h), w_down[1, f], NT)
+
+    each_chunk(hidden_back)
     scatter = attention(1, gather)
-    for f in range(2):
-        for copy in packed_copies(PACKED_BACK, 1, f, packed_back):
-            copy.wait_recv()
-    wait_expert_weights(1)
     spread = finish_attention(1, scatter)
     wait_all(spread)
-    for f in range(2):
-        pack(PACKED, 1, f, tokens, packed, False)
-    for f in range(2):
-        wait_all(packed_copies(PACKED, 1, f, packed))
-        block = feed_block(1, f)
-        gate_part = dot(block, w_gate[1, f])
-        up_part = dot(block, w_up[1, f])
-        back_hidden = dot(back_block(1, f), w_down[1, f], NT)
+    pack(PACKED, 1, tokens, packed, False)
+
+    def experts_both(f, h):
+        wait_all(packed_copies(PACKED, 1, f, h, packed))
+        gate_part, up_part = gate_and_up(1, f, h)
         to_gate, to_up = slopes_of(gate_part, up_part)
-        acts[2, f] = by_source(to_up * up_part)
-        expert_back(1, f, back_hidden, to_gate, to_up)
-    for f in range(2):
-        inner = acts[2, f].reshape(RING * group, hidden)
-        put_forward(1, f, inner)
+        acts[2, f, h] = (to_up * up_part).astype(BF16)
+        expert_back(1, f, h, slopes[0, f, h], to_gate, to_up)
+
+    each_chunk(experts_both)
+    each_chunk(lambda f, h: put_forward(1, f, h, acts[2, f, h]))
     expert_grads(1)
-    combine(RESULT_BACK, 1, result_back_send, result_back, False)
-    change = total_of_partials(start_partials(PARTIAL_BACK, partial_back), partial_back)
+    combine(RESULT_BACK, 1, packed_send, result_back, False)
+    copies = start_partials(PARTIAL_BACK, partial_back)
+    sum_cores(0)
+    start_ring(0)
+    change = total_of_partials(copies, partial_back)
 
     gather = start_back(1, cotangent[...], change)
     combine(RESULT, 1, result_send, result, True)
     late = start_partials(PARTIAL, partial)
-    sum_cores()
-    pl.semaphore_signal(credit, inc=1, device_id=core_device, device_id_type=MESH)
-    scatter = attention_back(1, gather)
+    sum_cores(1)
+    wait_all(gather)
+    start_ring(1)
+    pass_grads(0)
+    scatter = attention_back(1)
     proj_grads(1)
     ends_stage[0] = (middle[1] + total_of_partials(late, partial)).astype(BF16)
-    pass_grads()
+    sum_cores(2)
+    pl.semaphore_signal(credit, inc=1, device_id=core_device, device_id_type=MESH)
     incoming = finish_back(1, scatter)
     cotangent[...] = incoming.astype(F32)
 
     spread = spread_tokens(TOKENS_BACK, tokens_back, incoming)
+    start_ring(2)
+    pass_grads(1)
     proj_one()
-    for f in range(2):
-        block = feed_block(0, f)
-        gate_part = dot(block, w_gate[0, f])
-        up_part = dot(block, w_up[0, f])
+
+    def find_slopes(f, h):
+        gate_part, up_part = gate_and_up(0, f, h)
         to_gate, to_up = slopes_of(gate_part, up_part)
-        slopes[0, f] = to_gate
-        slopes[1, f] = to_up
-        acts[2, f] = by_source(to_up * up_part)
+        slopes[0, f, h] = to_gate
+        slopes[1, f, h] = to_up
+        acts[2, f, h] = (to_up * up_part).astype(BF16)
+
+    each_chunk(find_slopes)
     wait_all(spread)
-    for f in range(2):
-        pack(PACKED_BACK, 0, f, tokens_back, packed_back, True)
+    pack(PACKED_BACK, 0, tokens_back, packed_back, True)
+    pass_grads(2)
     proj_two(1)
-    for f in range(2):
-        wait_all(packed_copies(PACKED_BACK, 0, f, packed_back))
-        back_hidden = dot(back_block(0, f), w_down[0, f], NT)
-        expert_back(0, f, back_hidden, slopes[0, f], slopes[1, f])
-    finish_expert(1)
+
+    def experts_back(f, h):
+        wait_all(packed_copies(PACKED_BACK, 0, f, h, packed_back))
+        back_hidden = dot(back_chunk(0, f, h), w_down[0, f], NT)
+        expert_back(0, f, h, back_hidden, slopes[0, f, h], slopes[1, f, h])
+
+    each_chunk(experts_back)
+    for kind in range(3):
+        finish_expert(1, kind)
     for d in (1, -1):
         pl.semaphore_signal(y_credit, inc=1, device_id=y_device(d), device_id_type=MESH)
     pl.semaphore_wait(credit, 1)
     expert_grads(0)
     proj_three(1)
-    combine(RESULT_BACK, 0, result_back_send, result_back, False)
-    change = total_of_partials(start_partials(PARTIAL_BACK, partial_back), partial_back)
+    combine(RESULT_BACK, 0, packed_send, result_back, False)
+    copies = start_partials(PARTIAL_BACK, partial_back)
+    pl.semaphore_wait(y_credit, 2)
+    sum_cores(0)
+    start_ring(0)
+    change = total_of_partials(copies, partial_back)
     gather = start_back(0, cotangent[...], change)
-    pl.semaphore_wait(y_credit, 2)
-    sum_cores()
-    scatter = attention_back(0, gather)
+    sum_cores(1)
+    wait_all(gather)
+    start_ring(1)
+    pass_grads(0)
+    scatter = attention_back(0)
+
     @pl.when(core != 1)
     def _():
         out_proj(1).wait_send()
 
     proj_grads(0)
-    pass_grads()
+    sum_cores(2)
+    start_ring(2)
     ends_stage[1] = finish_back(0, scatter)
-    proj_one()
 
     ends_out[core] = jnp.where(first, ends_stage[1], ends_stage[0])
     ends_copy_out = core_copy(C_OUT_ENDS, ends_stage.at[core], ends_out.at[core])
     ends_copy_out.start()
     term_copy = core_copy(C_TERM, terms.at[other], terms_core)
     term_copy.start()
+    wait_out(1)
+    proj_one()
     term_copy.wait()
     terms_recv[0, 0] = terms[core] + terms_core[...]
     for axis, (row, device) in enumerate(
@@ -1018,11 +1054,15 @@
         for copy in copies:
             copy.start()
         if axis == 0:
+            pass_grads(1)
             proj_two(0)
         if axis == 1:
+            pass_grads(2)
             proj_three(0)
-        for copy in copies:
-            copy.wait()
+            finish_expert(0, 0)
+        if axis == 2:
+            finish_expert(0, 1)
+        wait_all(copies)
         total = terms_recv[axis, 0]
         for d in (1, 2, 3):
             total = total + terms_recv[axis, d]
@@ -1031,13 +1071,13 @@
         else:
             gains_out[...] = total
 
-    wait_out(1)
-    finish_expert(0)
+    finish_expert(0, 2)
     wait_out(0)
     for layer in range(2):
         @pl.when(core == layer)
         def _():
-            out_expert(layer).wait_recv()
+            for kind in range(3):
+                out_expert(layer, kind).wait_recv()
             out_proj(layer).wait_recv()
 
     @pl.when(core != 0)
@@ -1050,7 +1090,9 @@
     for copy in sent_weights():
         copy.wait_send()
     for layer in range(2):
-        weight_half(layer).wait_send()
+        for d in range(RING):
+            for i in range(RING):
+                weight_pass(layer, d, i).wait_send()
         for d in (1, 2, 3):
             weight_first(layer, d).wait_send()
             for i in range(RING):
@@ -1078,21 +1120,52 @@
     gate_out,
     up_out,
     down_out,
+    ends,
+    gains,
+    proj,
+    experts,
+    turned,
+    sems,
 ):
-    ends_out[0] = ends_ref[...]
-    attn_gain_out[...] = gains_ref[0:1]
-    feed_gain_out[...] = gains_ref[1:2]
-    query_gain_out[...] = exact_dot(gains_ref[2:3, : 4 * HEAD], copies_of_head(4), NT)
-    key_gain_out[...] = exact_dot(gains_ref[2:3, 4 * HEAD : 6 * HEAD], copies_of_head(2), NT)
+    pieces = [(kind, f) for kind in range(3) for f in range(2)]
+    moves = [
+        pltpu.make_async_copy(
+            experts_ref.at[kind, f], experts.at[kind, f], sems.at[2 * kind + f]
+        )
+        for kind, f in pieces
+    ]
+    moves += [
+        pltpu.make_async_copy(ends_ref, ends, sems.at[6]),
+        pltpu.make_async_copy(gains_ref, gains, sems.at[7]),
+        pltpu.make_async_copy(proj_ref, proj, sems.at[8]),
+    ]
+    for move in moves:
+        move.start()
+    results = []
+    for i, (kind, f) in enumerate(pieces):
+        moves[i].wait()
+        if kind < 2:
+            turned[kind, f] = experts[kind, f].T
+        source = experts.at[kind, f] if kind == 2 else turned.at[kind, f]
+        target = (gate_out, up_out, down_out)[kind]
+        results.append(pltpu.make_async_copy(source, target.at[0, f], sems.at[9 + i]))
+        results[-1].start()
+    moves[6].wait()
+    results.append(pltpu.make_async_copy(ends, ends_out.at[0], sems.at[15]))
+    results[-1].start()
+    moves[7].wait()
+    attn_gain_out[...] = gains[0:1]
+    feed_gain_out[...] = gains[1:2]
+    query_gain_out[...] = exact_dot(gains[2:3, : 4 * HEAD], copies_of_head(4), NT)
+    key_gain_out[...] = exact_dot(gains[2:3, 4 * HEAD : 6 * HEAD], copies_of_head(2), NT)
+    moves[8].wait()
     swap = swap_heads()
-    query_out[0] = exact_dot(proj_ref[0, :, : 4 * HEAD], swap)
-    key_out[0] = proj_ref[0, :, 4 * HEAD :]
-    value_out[0] = proj_ref[1, :, : 2 * HEAD]
-    out_out[0] = exact_dot(proj_ref[1, :, 2 * HEAD :], swap)
-    for f in range(2):
-        gate_out[0, f] = experts_ref[0, f].T
-        up_out[0, f] = experts_ref[1, f].T
-        down_out[0, f] = experts_ref[2, f]
+    query_out[0] = exact_dot(proj[0, :, : 4 * HEAD], swap)
+    key_out[0] = proj[0, :, 4 * HEAD :]
+    value_out[0] = proj[1, :, : 2 * HEAD]
+    out_out[0] = exact_dot(proj[1, :, 2 * HEAD :], swap)
+    for result in results:
+        result.wait()
 
 
 def shards(
@@ -1119,6 +1192,8 @@
     experts_all = w_gate.shape[1] * lax.axis_size("expert")
     capacity = 3 * rows * top // (2 * experts_all)
     group = RING * capacity
+    part_rows = group // 2
+    chunk = RING * part_rows
     span = RING * rows
     vmem = pl.BlockSpec(memory_space=pltpu.VMEM)
     anywhere = pl.BlockSpec(memory_space=pl.ANY)
@@ -1151,22 +1226,21 @@
         pltpu.VMEM((RING - 1, rows, width), BF16),
         pltpu.VMEM((RING, rows, width), BF16),
         pltpu.VMEM((RING, rows, width), BF16),
-        pltpu.VMEM((2, RING - 1, group, width), BF16),
-        pltpu.VMEM((2, 2, RING, group, width), BF16),
-        pltpu.VMEM((2, 2, RING, group, width), BF16),
-        pltpu.VMEM((2, RING - 1, group, width), BF16),
-        pltpu.VMEM((2, RING, group, width), BF16),
-        pltpu.VMEM((2, RING - 1, group, width), BF16),
-        pltpu.VMEM((2, RING, group, width), BF16),
+        pltpu.VMEM((2, 2, RING - 1, group // 2, width), BF16),
+        pltpu.VMEM((2, 2, 2, RING, group // 2, width), BF16),
+        pltpu.VMEM((2, 2, 2, RING, group // 2, width), BF16),
+        pltpu.VMEM((2, 2, RING - 1, group // 2, width), BF16),
+        pltpu.VMEM((2, 2, RING, group // 2, width), BF16),
+        pltpu.VMEM((2, 2, RING, group // 2, width), BF16),
         pltpu.VMEM((RING, rows, width), BF16),
         pltpu.VMEM((RING - 1, rows, width), BF16),
         pltpu.VMEM((RING - 1, rows, width), BF16),
         pltpu.VMEM((span, width), F32),
-        pltpu.VMEM((2, 2, RING * group, hidden), F32),
+        pltpu.VMEM((2, 2, 2, 2 * group, hidden), F32),
         pltpu.VMEM((2, RING, rows, width), BF16),
         pltpu.VMEM((span, half), BF16),
         pltpu.VMEM((span, 2 * HEAD), BF16),
-        pltpu.VMEM((3, 2, RING, group, hidden), BF16),
+        pltpu.VMEM((3, 2, 2, 2 * group, hidden), BF16),
         pltpu.VMEM((2, 3, RING, hidden // RING, width), BF16),
         pltpu.VMEM((3, RING, hidden // RING, width), BF16),
         pltpu.VMEM((3, 6, rows, width), BF16),
@@ -1185,6 +1259,8 @@
         pltpu.SemaphoreType.DMA((RING_ROWS, RING - 1)),
         pltpu.SemaphoreType.DMA((2, RING - 1, RING)),
         pltpu.SemaphoreType.DMA((2, RING - 1, RING)),
+        pltpu.SemaphoreType.DMA((2, RING, RING)),
+        pltpu.SemaphoreType.DMA((2, RING, RING)),
         pltpu.SemaphoreType.DMA((RING - 1, RING)),
         pltpu.SemaphoreType.DMA((RING - 1, RING)),
         pltpu.SemaphoreType.DMA((3, 6)),
@@ -1192,7 +1268,7 @@
         pltpu.SemaphoreType.DMA((CORE_ROWS,)),
         pltpu.SemaphoreType.DMA((CORE_ROWS,)),
         pltpu.SemaphoreType.DMA((3,)),
-        pltpu.SemaphoreType.DMA,
+        pltpu.SemaphoreType.DMA((3,)),
         pltpu.SemaphoreType.REGULAR,
         pltpu.SemaphoreType.REGULAR,
     ]
@@ -1208,7 +1284,7 @@
         out_specs=(vmem, vmem, vmem, anywhere),
         scratch_shapes=scratch,
         compiler_params=pltpu.CompilerParams(
-            collective_id=0, has_side_effects=True, vmem_limit_bytes=62 << 20
+            collective_id=0, has_side_effects=True, vmem_limit_bytes=63 << 20
         ),
         cost_estimate=pl.CostEstimate(
             flops=60_000_000_000, bytes_accessed=20_000_000, transcendentals=4_000_000
@@ -1248,9 +1324,17 @@
     outputs = pl.pallas_call(
         finish,
         out_shape=tuple(jax.ShapeDtypeStruct(shape, dtype) for shape, dtype in shapes),
-        in_specs=[vmem] * 4,
-        out_specs=(vmem,) * len(shapes),
-        compiler_params=pltpu.CompilerParams(vmem_limit_bytes=32 << 20),
+        in_specs=[anywhere] * 4,
+        out_specs=(anywhere,) + (vmem,) * 8 + (anywhere,) * 3,
+        scratch_shapes=[
+            pltpu.VMEM((2, rows, width), BF16),
+            pltpu.VMEM((8, width), F32),
+            pltpu.VMEM((2, rows, half), F32),
+            pltpu.VMEM((3, 2, hidden // RING, width), F32),
+            pltpu.VMEM((2, 2, width, hidden // RING), F32),
+            pltpu.SemaphoreType.DMA((16,)),
+        ],
+        compiler_params=pltpu.CompilerParams(vmem_limit_bytes=60 << 20),
         name="finish",
     )(ends, gain_sums, proj, experts)
     return (*outputs[:8], outputs[8].transpose(0, 2, 1), *outputs[9:])

time: 256 us -> 235 us (0.918)
  Pallas kernels: 250 us -> 234 us
  local copies, waits for them, and re-layouts: 4.52 us -> 0 us
    pallas_call x1, Pallas kernels: 248 us -> 230 us  [shards(): pl.pallas_call(functools.partial(kernel, rows, width, hidden, capacity),...]
    unnamed x8 -> x0, local copies, waits for them, and re-layouts: 4.52 us -> none
where the time goes in v1:
time: 235 us
  Pallas kernels  234 us (100%)
    pallas_call x1, Pallas kernels, shards(): pl.pallas_call(functools.partial(kernel, rows, width, hidden, capacity),...  230 us

profile of v1, /device:TPU:0, one launch (start us, length us, event | category | flops | bytes accessed | tf_op | source)
XLA Modules:
  0.0 235.2 jit_solution(1227142371313549142)
XLA Ops:
  0.7 230.4 %layers.1 = (bf16[2,64,1024]{2,1,0:T(8,128)(2,1)}, f32[8,1024]{1,0:T(8,128)}, f32[2,64,384]{2,1,0:T(8,128)}, f32[3,2,128,1024]{3,2,1,0:T(8,128)}) custom-call(bf16[2,64,1024]{2,1,0:T(8,128)(2,1)} %bitcast.20, s32[2,256]{1,0:T(2,128)} %segments_ref.1, s32[2,8,64]{2,1,0:T(8,128)} %bitcast.26, f32[2,8,64]{2,1,0:T(8,128)} %bitcast.27, f32[1,1024]{1,0:T(1,128)} %attn_gain_ref.1, ...), custom_call_target="tpu_custom_call" | custom-call | flops 60000002048 | bytes 20000000 | tf_op jit(solution)/shard_map/layers/pallas_call | solution.py:1275
  231.1 3.9 %finish.1 = (bf16[1,2,64,1024]{3,2,1,0:T(8,128)(2,1)}, f32[1,1024]{1,0:T(1,128)}, f32[1,64]{1,0:T(1,128)}, f32[1,64]{1,0:T(1,128)}, f32[1,1024]{1,0:T(1,128)}, /...) custom-call(bf16[2,64,1024]{2,1,0:T(8,128)(2,1)} %get-tuple-element., ...), custom_call_target="tpu_custom_call" | custom-call | tf_op jit(solution)/shard_map/finish/pallas_call | solution.py:1324

commit v2 on v1

--- a/solution.py
+++ b/solution.py
@@ -19,10 +19,11 @@
 NT = (((1,), (1,)), ((), ()))
 TN = (((0,), (0,)), ((), ()))
 
-Y_GATHER, Y_SUM, Y_GATHER_BACK, Y_SUM_BACK, TOKENS, TOKENS_BACK = range(6)
-PARTIAL, PARTIAL_BACK, GRAD_Q, GAIN_P, GAIN_Q, GAIN_Y = 6, 7, 8, 10, 11, 12
-WEIGHT_P, TABLE_P = 13, 15
-PACKED, PACKED_BACK, RESULT, RESULT_BACK, RING_ROWS = 16, 20, 24, 28, 32
+PIECES = 4
+Y_GATHER, Y_SUM, Y_GATHER_BACK, Y_SUM_BACK = 0, 4, 8, 12
+TOKENS, TOKENS_BACK, PARTIAL, PARTIAL_BACK = 16, 20, 24, 28
+GRAD_Q, GAIN_P, GAIN_Q, GAIN_Y, WEIGHT_P, TABLE_P = 32, 34, 35, 36, 37, 39
+PACKED, PACKED_BACK, RESULT, RESULT_BACK, RING_ROWS = 40, 44, 48, 52, 56
 
 C_ENDS, C_GAINS, C_ROUTES, C_GATES, C_PIECE = range(5)
 C_GATE, C_UP, C_DOWN, C_GRAD, C_PROJ, C_TERM, C_OUT_ENDS = 5, 6, 7, 8, 11, 12, 13
@@ -122,7 +123,7 @@
     parts,
     slopes,
     attn_back,
-    back_qk,
+    low_qk,
     back_v,
     acts,
     grads,
@@ -186,6 +187,9 @@
 
     core_device = (other, place, shard)
 
+    def order(k):
+        return k + lax.div(k, 2) * (5 - 2 * k)
+
     def ring_copy(row, d, src, dst, device):
         return pltpu.make_async_remote_copy(
             src_ref=src,
@@ -386,9 +390,6 @@
     def qk_gain(layer):
         return gains[layer, 2:3, : 6 * HEAD]
 
-    def allowed():
-        return mask_ref[...] != 0.0
-
     def normed_qk(layer):
         raw = raw_qk[layer]
         scale = lax.rsqrt(head_mean(raw * raw) + EPS)
@@ -396,14 +397,19 @@
         low = (normed * qk_gain(layer)).astype(BF16)
         return low, normed, scale
 
-    def probs_of(low, tile, half, mask):
-        query = low[:, tile * 2 * HEAD : (tile + 1) * 2 * HEAD]
-        key = low[:, 4 * HEAD :]
-        query = jnp.where(halves[half], query, jnp.zeros_like(query))
+    def head_columns(tile):
+        return slice(tile * 2 * HEAD, (tile + 1) * 2 * HEAD)
+
+    def block_rows(block):
+        return pl.ds(pl.multiple_of(block * rows, rows), rows)
+
+    def one_half(block, half):
+        return jnp.where(halves[half], block, jnp.zeros_like(block))
+
+    def exp_scores(query, key, mask):
         scores = dot(query, key, NT) * HEAD ** (-0.5)
-        scores = jnp.where(mask, scores, NEG)
-        expo = jnp.exp(scores - jnp.max(scores, axis=-1, keepdims=True))
-        return expo / jnp.sum(expo, axis=-1, keepdims=True), query, key
+        expo = jnp.exp(jnp.where(mask != 0.0, scores, NEG))
+        return expo, 1.0 / jnp.sum(expo, axis=-1, keepdims=True)
 
     half_rows = (slice(0, 8), slice(8, 16))
 
@@ -411,40 +417,49 @@
         block = w_attn[layer, half, places, :, start * HEAD : stop * HEAD]
         return block.reshape(block.shape[0] * rows, (stop - start) * HEAD)
 
-    def y_gather(row, buffer, layer):
-        copies = [
-            ring_copy(row, d, buffer.at[layer, shard], buffer.at[layer, shard], y_device(d))
-            for d in (1, 3, 2)
-        ]
-        for copy in copies:
-            copy.start()
-        return copies
+    row_halves = tuple(pl.ds(i * rows // PIECES, rows // PIECES) for i in range(PIECES))
+
+    def y_gather_copy(row, d, h, buffer, layer):
+        held = buffer.at[layer, shard, row_halves[h]]
+        return ring_copy(row + h, d, held, held, y_device(d))
+
+    def start_gather(row, h, buffer, layer):
+        for d in (1, 3, 2):
+            y_gather_copy(row, d, h, buffer, layer).start()
+
+    def y_scatter_copy(row, d, h):
+        cut = row_halves[h]
+        return ring_copy(
+            row + h, d, y_send.at[mod(shard + d), cut], y_recv.at[d - 1, cut], y_device(d)
+        )
 
     def y_scatter(row):
-        copies = [
-            ring_copy(row, d, y_send.at[mod(shard + d)], y_recv.at[d - 1], y_device(d))
-            for d in (1, 3, 2)
-        ]
-        for copy in copies:
-            copy.start()
-        return copies
-
-    def y_total(copies):
-        for copy in copies:
-            copy.wait()
-        total = y_send[shard].astype(F32)
+        for h in range(len(row_halves)):
+            for d in (1, 3, 2):
+                y_scatter_copy(row, d, h).start()
+
+    def y_total(row, h):
+        cut = row_halves[h]
+        for d in (1, 3, 2):
+            y_scatter_copy(row, d, h).wait()
+        total = y_send[shard, cut].astype(F32)
         for d in (1, 2, 3):
-            total = total + y_recv[d - 1].astype(F32)
+            total = total + y_recv[d - 1, cut].astype(F32)
         return total
 
-    def spread_tokens(row, buffer, block):
-        buffer[p] = block
-        copies = [
-            ring_copy(row, d, buffer.at[p], buffer.at[p], p_device(d)) for d in (1, 3, 2)
-        ]
-        for copy in copies:
-            copy.start()
-        return copies
+    def spread_copy(row, buffer, d, h):
+        held = buffer.at[p, row_halves[h]]
+        return ring_copy(row + h, d, held, held, p_device(d))
+
+    def spread_half(row, buffer, h, block):
+        buffer[p, row_halves[h]] = block
+        for d in (1, 3, 2):
+            spread_copy(row, buffer, d, h).start()
+
+    def wait_spread(row, buffer):
+        for h in range(len(row_halves)):
+            for d in (1, 3, 2):
+                spread_copy(row, buffer, d, h).wait()
 
     column_halves = (pl.ds(0, width // 2), pl.ds(width // 2, width // 2))
 
@@ -545,26 +560,24 @@
         for i in range(RING):
             partial_send[i] = parts[i * rows : (i + 1) * rows].astype(BF16)
 
-    def partial_copies(row, target):
-        return [
-            ring_copy(
-                row, d, partial_send.at[mod(p + d)], target.at[d - 1], p_device(d)
-            )
-            for d in (1, 3, 2)
-        ]
+    def partial_copy(row, target, d, h):
+        cut = row_halves[h]
+        return ring_copy(
+            row + h, d, partial_send.at[mod(p + d), cut], target.at[d - 1, cut], p_device(d)
+        )
 
     def start_partials(row, target):
-        copies = partial_copies(row, target)
-        for copy in copies:
-            copy.start()
-        return copies
-
-    def total_of_partials(copies, target):
-        for copy in copies:
-            copy.wait()
-        total = partial_send[p].astype(F32)
+        for h in range(len(row_halves)):
+            for d in (1, 3, 2):
+                partial_copy(row, target, d, h).start()
+
+    def total_of_partials(row, target, h):
+        cut = row_halves[h]
+        for d in (1, 3, 2):
+            partial_copy(row, target, d, h).wait()
+        total = partial_send[p, cut].astype(F32)
         for d in (1, 2, 3):
-            total = total + target[d - 1].astype(F32)
+            total = total + target[d - 1, cut].astype(F32)
         return total
 
     def wait_expert_weights(layer):
@@ -582,38 +595,51 @@
         for copy in copies:
             copy.wait()
 
-    def start_attention(layer):
-        held = stream[layer]
-        attn_all[layer, shard] = (held * scale_of(held) * gains[layer, 0:1, :]).astype(BF16)
-        return y_gather(Y_GATHER, attn_all, layer)
-
-    def attention(layer, copies):
-        wait_all(copies)
+    def start_attention(layer, h):
+        cut = row_halves[h]
+        held = stream[layer, cut]
+        attn_all[layer, shard, cut] = (
+            held * scale_of(held) * gains[layer, 0:1, :]
+        ).astype(BF16)
+        start_gather(Y_GATHER, h, attn_all, layer)
+
+    def attention(layer):
+        for h in range(len(row_halves)):
+            for d in (1, 3, 2):
+                y_gather_copy(Y_GATHER, d, h, attn_all, layer).wait()
         whole = attn_all[layer].reshape(span, width)
         raw_qk[layer] = dot(whole, weight_of(layer, 0, 0, 6))
         values[layer] = dot(whole, weight_of(layer, 1, 0, 2)).astype(BF16)
-        low, _n, _s = normed_qk(layer)
-        mask = allowed()
+        low_qk[...] = normed_qk(layer)[0]
+
+        key = low_qk[:, head_columns(2)]
         value = values[layer]
-        for tile in range(2):
-            halves_out = []
-            for half in range(2):
-                probs, _q, _k = probs_of(low, tile, half, mask)
-                halves_out.append(dot(probs.astype(BF16), value))
-            mixed[layer, :, tile * 2 * HEAD : (tile + 1) * 2 * HEAD] = jnp.where(
-                low_half, halves_out[0], halves_out[1]
-            ).astype(BF16)
-        for places, cut in zip(half_rows, column_halves):
-            out = dot(mixed[layer], weight_of(layer, 1, 2, 6, places), NT)
-            for i in range(RING):
-                y_send[i, :, cut] = out[i * rows : (i + 1) * rows].astype(BF16)
-        return y_scatter(Y_SUM)
-
-    def finish_attention(layer, copies):
-        center = stream[layer] + y_total(copies)
-        middle[layer] = center
-        feed = (center * scale_of(center) * gains[layer, 1:2, :]).astype(BF16)
-        return spread_tokens(TOKENS, tokens, feed)
+        for group_of in ((2, 1, 3, 0),):
+            blocks = [mod(shard + d) for d in group_of]
+            cuts = [block_rows(block) for block in blocks]
+            mask = jnp.concatenate([mask_ref[cut] for cut in cuts], axis=0)
+            tiles = []
+            for tile in range(2):
+                query = jnp.concatenate([low_qk[cut, head_columns(tile)] for cut in cuts], axis=0)
+                outs = []
+                for half in range(2):
+                    expo, share = exp_scores(one_half(query, half), key, mask)
+                    outs.append(dot((expo * share).astype(BF16), value))
+                tiles.append(jnp.where(low_half, outs[0], outs[1]).astype(BF16))
+            whole_mixed = jnp.concatenate(tiles, axis=1)
+            out = dot(whole_mixed, weight_of(layer, 1, 2, 6), NT).astype(BF16)
+            for i, (d, block, cut) in enumerate(zip(group_of, blocks, cuts)):
+                part = slice(i * rows, (i + 1) * rows)
+                mixed[layer, cut] = whole_mixed[part]
+                y_send[block] = out[part]
+        y_scatter(Y_SUM)
+
+    def finish_attention(layer):
+        for h, cut in enumerate(row_halves):
+            center = stream[layer, cut] + y_total(Y_SUM, h)
+            middle[layer, cut] = center
+            feed = center * scale_of(center) * gains[layer, 1:2, :]
+            spread_half(TOKENS, tokens, h, feed.astype(BF16))
 
     def feed_block(layer, f):
         return packed[layer, f].reshape(RING * group, width)
@@ -792,53 +818,84 @@
             proj_stage[...] = total
             out_proj(layer).start()
 
-    def start_back(layer, incoming, change):
-        center = middle[layer]
-        scale = scale_of(center)
-        normed = center * scale
-        terms[layer, 1:2] = jnp.sum(change * normed, axis=0, keepdims=True)
-        scaled = change * gains[layer, 1:2, :]
-        inner = jnp.mean(scaled * normed, axis=-1, keepdims=True)
-        back_mid = incoming + scale * (scaled - normed * inner)
-        cotangent[...] = back_mid
-        attn_back[layer, shard] = back_mid.astype(BF16)
-        return y_gather(Y_GATHER_BACK, attn_back, layer)
+    def start_back(layer):
+        for h, cut in enumerate(row_halves):
+            change = total_of_partials(PARTIAL_BACK, partial_back, h)
+            center = middle[layer, cut]
+            scale = scale_of(center)
+            normed = center * scale
+            terms[layer, 1:2] += jnp.sum(change * normed, axis=0, keepdims=True)
+            scaled = change * gains[layer, 1:2, :]
+            inner = jnp.mean(scaled * normed, axis=-1, keepdims=True)
+            back_mid = cotangent[cut] + scale * (scaled - normed * inner)
+            cotangent[cut] = back_mid
+            attn_back[layer, shard, cut] = back_mid.astype(BF16)
+            start_gather(Y_GATHER_BACK, h, attn_back, layer)
+
+    def find_probs(layer):
+        low_qk[...] = normed_qk(layer)[0]
+        key = low_qk[:, head_columns(2)]
+        for i in range(4):
+            query = one_half(low_qk[:, head_columns(i // 2)], i % 2)
+            expo, share = exp_scores(query, key, mask_ref[...])
+            parts[:, i * span : (i + 1) * span] = expo * share
+
+    def change_at(block, columns):
+        return slopes.at[0, lax.div(block, 2), lax.rem(block, 2), pl.ds(0, rows), columns]
 
     def attention_back(layer):
-        low, normed, scale = normed_qk(layer)
-        whole_back = attn_back[layer].reshape(span, width)
-        back_mixed = dot(whole_back, weight_of(layer, 1, 2, 6)).astype(BF16)
+        key = low_qk[:, head_columns(2)]
         value = values[layer]
-        mask = allowed()
         back_key = jnp.zeros((span, 2 * HEAD), F32)
         back_value = jnp.zeros((span, 2 * HEAD), F32)
-        tiles = []
-        for tile in range(2):
-            pieces = []
-            for half in range(2):
-                probs, query, key = probs_of(low, tile, half, mask)
-                piece = back_mixed[:, tile * 2 * HEAD : (tile + 1) * 2 * HEAD]
-                piece = jnp.where(halves[half], piece, jnp.zeros_like(piece))
-                back_probs = dot(piece, value, NT)
-                back_value = back_value + dot(probs.astype(BF16), piece, TN)
-                total = jnp.sum(probs * back_probs, axis=-1, keepdims=True)
-                back_scores = (probs * (back_probs - total)).astype(BF16)
-                pieces.append(dot(back_scores, key))
-                back_key = back_key + dot(back_scores, query, TN)
-            tiles.append(jnp.where(low_half, pieces[0], pieces[1]))
-        change = jnp.concatenate(tiles + [back_key], axis=1) * HEAD ** (-0.5)
+        for group_of in ((0, 1, 3, 2),):
+            blocks = [mod(shard - d) for d in group_of]
+            cuts = [block_rows(block) for block in blocks]
+            for d in group_of:
+                for h in range(len(row_halves)):
+                    if d:
+                        y_gather_copy(Y_GATHER_BACK, d, h, attn_back, layer).wait()
+            back = jnp.concatenate([attn_back[layer, block] for block in blocks], axis=0)
+            back = dot(back, weight_of(layer, 1, 2, 6)).astype(BF16)
+            for tile in range(2):
+                pieces = []
+                queries = jnp.concatenate(
+                    [low_qk[cut, head_columns(tile)] for cut in cuts], axis=0
+                )
+                for half in range(2):
+                    i = 2 * tile + half
+                    columns = slice(i * span, (i + 1) * span)
+                    probs = jnp.concatenate([parts[cut, columns] for cut in cuts], axis=0)
+                    query = one_half(queries, half)
+                    piece = one_half(back[:, head_columns(tile)], half)
+                    back_probs = dot(piece, value, NT)
+                    back_value = back_value + dot(probs.astype(BF16), piece, TN)
+                    total = jnp.sum(probs * back_probs, axis=-1, keepdims=True)
+                    back_scores = (probs * (back_probs - total)).astype(BF16)
+                    pieces.append(dot(back_scores, key))
+                    back_key = back_key + dot(back_scores, query, TN)
+                joined = jnp.where(low_half, pieces[0], pieces[1])
+                for i, block in enumerate(blocks):
+                    change_at(block, pl.ds(tile * 2 * HEAD, 2 * HEAD))[...] = joined[
+                        i * rows : (i + 1) * rows
+                    ]
+        _low, normed, scale = normed_qk(layer)
+        change = jnp.concatenate(
+            [change_at(i, pl.ds(0, 4 * HEAD))[...] for i in range(RING)], axis=0
+        )
+        change = jnp.concatenate([change, back_key], axis=1) * HEAD ** (-0.5)
         term = jnp.sum(change * normed, axis=0, keepdims=True)
         terms[layer, 2:3, : 6 * HEAD] = term
         scaled = change * qk_gain(layer)
         inner = head_mean(scaled * normed)
-        back_qk[...] = (scale * (scaled - normed * inner)).astype(BF16)
+        low_qk[...] = (scale * (scaled - normed * inner)).astype(BF16)
         back_v[...] = back_value.astype(BF16)
         for places, cut in zip(half_rows, column_halves):
-            out = dot(back_qk[...], weight_of(layer, 0, 0, 6, places), NT)
+            out = dot(low_qk[...], weight_of(layer, 0, 0, 6, places), NT)
             out = out + dot(back_v[...], weight_of(layer, 1, 0, 2, places), NT)
             for i in range(RING):
                 y_send[i, :, cut] = out[i * rows : (i + 1) * rows].astype(BF16)
-        return y_scatter(Y_SUM_BACK)
+        y_scatter(Y_SUM_BACK)
 
     def proj_grads(layer):
         def step(i, _):
@@ -847,7 +904,7 @@
             feed = attn_all[layer, :, :, cut].reshape(span, 4 * rows)
             back = attn_back[layer, :, :, cut].reshape(span, 4 * rows)
             for half, start, stop, lhs, rhs in (
-                (0, 0, 6, feed, back_qk[...]),
+                (0, 0, 6, feed, low_qk[...]),
                 (1, 0, 2, feed, back_v[...]),
                 (1, 2, 6, back, mixed[layer]),
             ):
@@ -860,15 +917,16 @@
         lax.fori_loop(0, 4, step, 0)
         proj_core_copy().start()
 
-    def finish_back(layer, copies):
-        total = y_total(copies)
-        held = stream[layer]
-        scale = scale_of(held)
-        normed = held * scale
-        terms[layer, 0:1] = jnp.sum(total * normed, axis=0, keepdims=True)
-        scaled = total * gains[layer, 0:1, :]
-        inner = jnp.mean(scaled * normed, axis=-1, keepdims=True)
-        return (cotangent[...] + scale * (scaled - normed * inner)).astype(BF16)
+    def finish_back(layer, take):
+        for h, cut in enumerate(row_halves):
+            total = y_total(Y_SUM_BACK, h)
+            held = stream[layer, cut]
+            scale = scale_of(held)
+            normed = held * scale
+            terms[layer, 0:1] += jnp.sum(total * normed, axis=0, keepdims=True)
+            scaled = total * gains[layer, 0:1, :]
+            inner = jnp.mean(scaled * normed, axis=-1, keepdims=True)
+            take(h, cut, (cotangent[cut] + scale * (scaled - normed * inner)).astype(BF16))
 
     def slopes_of(gate_part, up_part):
         sigmoid = jax.nn.sigmoid(gate_part)
@@ -898,20 +956,22 @@
         block = feed_chunk(layer, f, h)
         return dot(block, w_gate[layer, f]), dot(block, w_up[layer, f])
 
-    gather = start_attention(0)
+    for h in range(len(row_halves)):
+        start_attention(0, h)
     start_second(0)
     make_tables()
-    early = spread_tokens(TOKENS_BACK, tokens_back, cotangent[...].astype(BF16))
+    for h, cut in enumerate(row_halves):
+        spread_half(TOKENS_BACK, tokens_back, h, cotangent[cut].astype(BF16))
     start_pass(0)
     for copy in sent_weights():
         copy.start()
     wait_pass(0)
-    scatter = attention(0, gather)
+    attention(0)
     start_second(1)
     take_tables()
-    wait_all(early)
+    wait_spread(TOKENS_BACK, tokens_back)
     pack(PACKED_BACK, 1, tokens_back, packed_back, True)
-    spread = finish_attention(0, scatter)
+    finish_attention(0)
     start_pass(1)
 
     def packed_back_sent(f, h):
@@ -920,7 +980,7 @@
 
     each_chunk(packed_back_sent)
     wait_expert_weights(0)
-    wait_all(spread)
+    wait_spread(TOKENS, tokens)
     pack(PACKED, 0, tokens, packed, False)
 
     def experts_forward(f, h):
@@ -931,10 +991,12 @@
 
     each_chunk(experts_forward)
     combine(RESULT, 0, result_send, result, True)
-    final = middle[0] + total_of_partials(start_partials(PARTIAL, partial), partial)
-    stream[1] = final.astype(BF16).astype(F32)
-
-    gather = start_attention(1)
+    start_partials(PARTIAL, partial)
+    for h, cut in enumerate(row_halves):
+        final = middle[0, cut] + total_of_partials(PARTIAL, partial, h)
+        stream[1, cut] = final.astype(BF16).astype(F32)
+        start_attention(1, h)
+
     wait_pass(1)
     wait_expert_weights(1)
 
@@ -944,9 +1006,9 @@
         slopes[0, f, h] = dot(back_chunk(1, f, h), w_down[1, f], NT)
 
     each_chunk(hidden_back)
-    scatter = attention(1, gather)
-    spread = finish_attention(1, scatter)
-    wait_all(spread)
+    attention(1)
+    finish_attention(1)
+    wait_spread(TOKENS, tokens)
     pack(PACKED, 1, tokens, packed, False)
 
     def experts_both(f, h):
@@ -960,29 +1022,32 @@
     each_chunk(lambda f, h: put_forward(1, f, h, acts[2, f, h]))
     expert_grads(1)
     combine(RESULT_BACK, 1, packed_send, result_back, False)
-    copies = start_partials(PARTIAL_BACK, partial_back)
+    start_partials(PARTIAL_BACK, partial_back)
     sum_cores(0)
     start_ring(0)
-    change = total_of_partials(copies, partial_back)
-
-    gather = start_back(1, cotangent[...], change)
+
+    start_back(1)
     combine(RESULT, 1, result_send, result, True)
-    late = start_partials(PARTIAL, partial)
+    start_partials(PARTIAL, partial)
     sum_cores(1)
-    wait_all(gather)
-    start_ring(1)
+    find_probs(1)
     pass_grads(0)
-    scatter = attention_back(1)
+    attention_back(1)
     proj_grads(1)
-    ends_stage[0] = (middle[1] + total_of_partials(late, partial)).astype(BF16)
+    for h, cut in enumerate(row_halves):
+        final = middle[1, cut] + total_of_partials(PARTIAL, partial, h)
+        ends_stage[0, cut] = final.astype(BF16)
     sum_cores(2)
     pl.semaphore_signal(credit, inc=1, device_id=core_device, device_id_type=MESH)
-    incoming = finish_back(1, scatter)
-    cotangent[...] = incoming.astype(F32)
-
-    spread = spread_tokens(TOKENS_BACK, tokens_back, incoming)
+
+    def hand_on(h, cut, block):
+        cotangent[cut] = block.astype(F32)
+        spread_half(TOKENS_BACK, tokens_back, h, block)
+
+    finish_back(1, hand_on)
+
+    start_ring(1)
     start_ring(2)
-    pass_grads(1)
     proj_one()
 
     def find_slopes(f, h):
@@ -993,8 +1058,9 @@
         acts[2, f, h] = (to_up * up_part).astype(BF16)
 
     each_chunk(find_slopes)
-    wait_all(spread)
+    wait_spread(TOKENS_BACK, tokens_back)
     pack(PACKED_BACK, 0, tokens_back, packed_back, True)
+    pass_grads(1)
     pass_grads(2)
     proj_two(1)
 
@@ -1012,17 +1078,16 @@
     expert_grads(0)
     proj_three(1)
     combine(RESULT_BACK, 0, packed_send, result_back, False)
-    copies = start_partials(PARTIAL_BACK, partial_back)
+    start_partials(PARTIAL_BACK, partial_back)
     pl.semaphore_wait(y_credit, 2)
     sum_cores(0)
     start_ring(0)
-    change = total_of_partials(copies, partial_back)
-    gather = start_back(0, cotangent[...], change)
+    start_back(0)
     sum_cores(1)
-    wait_all(gather)
+    find_probs(0)
+    pass_grads(0)
+    attention_back(0)
     start_ring(1)
-    pass_grads(0)
-    scatter = attention_back(0)
 
     @pl.when(core != 1)
     def _():
@@ -1031,7 +1096,11 @@
     proj_grads(0)
     sum_cores(2)
     start_ring(2)
-    ends_stage[1] = finish_back(0, scatter)
+
+    def keep(h, cut, block):
+        ends_stage[1, cut] = block
+
+    finish_back(0, keep)
 
     ends_out[core] = jnp.where(first, ends_stage[1], ends_stage[0])
     ends_copy_out = core_copy(C_OUT_ENDS, ends_stage.at[core], ends_out.at[core])

time: 235 us -> 218 us (0.928)
  Pallas kernels: 234 us -> 217 us
    pallas_call x1, Pallas kernels: 230 us -> 213 us  [shards(): pl.pallas_call(functools.partial(kernel, rows, width, hidden, capacity),...]
where the time goes in v2:
time: 218 us
  Pallas kernels  217 us (100%)
    pallas_call x1, Pallas kernels, shards(): pl.pallas_call(functools.partial(kernel, rows, width, hidden, capacity),...  213 us

profile of v2, /device:TPU:0, one launch (start us, length us, event | category | flops | bytes accessed | tf_op | source)
XLA Modules:
  0.0 218.1 jit_solution(11258099589610619357)
XLA Ops:
  0.7 213.4 %layers.1 = (bf16[2,64,1024]{2,1,0:T(8,128)(2,1)}, f32[8,1024]{1,0:T(8,128)}, f32[2,64,384]{2,1,0:T(8,128)}, f32[3,2,128,1024]{3,2,1,0:T(8,128)}) custom-call(bf16[2,64,1024]{2,1,0:T(8,128)(2,1)} %bitcast.20, s32[2,256]{1,0:T(2,128)} %segments_ref.1, s32[2,8,64]{2,1,0:T(8,128)} %bitcast.26, f32[2,8,64]{2,1,0:T(8,128)} %bitcast.27, f32[1,1024]{1,0:T(1,128)} %attn_gain_ref.1, ...), custom_call_target="tpu_custom_call" | custom-call | flops 60000002048 | bytes 20000000 | tf_op jit(solution)/shard_map/layers/pallas_call | solution.py:1344
  214.0 3.9 %finish.1 = (bf16[1,2,64,1024]{3,2,1,0:T(8,128)(2,1)}, f32[1,1024]{1,0:T(1,128)}, f32[1,64]{1,0:T(1,128)}, f32[1,64]{1,0:T(1,128)}, f32[1,1024]{1,0:T(1,128)}, /...) custom-call(bf16[2,64,1024]{2,1,0:T(8,128)(2,1)} %get-tuple-element., ...), custom_call_target="tpu_custom_call" | custom-call | tf_op jit(solution)/shard_map/finish/pallas_call | solution.py:1393

commit v3 on v2

--- a/solution.py
+++ b/solution.py
@@ -294,20 +294,20 @@
         )
 
     def start_first(layer):
-        for d in (1, 3, 2):
+        for d in (2, 1, 3):
             weight_first(layer, d).start()
 
     def start_second(layer):
         for i in (0, 1, 3, 2):
             if i:
                 weight_first(layer, i).wait_recv()
-            for d in (1, 3, 2):
+            for d in (2, 1, 3):
                 weight_second(layer, d, i).start()
             weight_pass(layer, 0, i).start()
 
     def start_pass(layer):
         for i in (0, 1, 3, 2):
-            for d in (1, 3, 2):
+            for d in (2, 1, 3):
                 weight_second(layer, d, i).wait_recv()
                 weight_pass(layer, d, i).start()
 
@@ -351,13 +351,13 @@
                 choose = (col_at == 2 * owner + lax.rem(row_at, 2)).astype(F32)
                 table_send[d, layer, 0] = exact_dot(choose, wide_slot)
                 table_send[d, layer, 1] = exact_dot(choose, wide_gate)
-        for d in (1, 3, 2):
+        for d in (2, 1, 3):
             ring_copy(
                 TABLE_P, d, table_send.at[d], table_recv.at[d - 1], p_device(d)
             ).start()
 
     def take_tables():
-        for d in (1, 3, 2):
+        for d in (2, 1, 3):
             ring_copy(
                 TABLE_P, d, table_send.at[d], table_recv.at[d - 1], p_device(d)
             ).wait_recv()
@@ -424,7 +424,7 @@
         return ring_copy(row + h, d, held, held, y_device(d))
 
     def start_gather(row, h, buffer, layer):
-        for d in (1, 3, 2):
+        for d in (2, 1, 3):
             y_gather_copy(row, d, h, buffer, layer).start()
 
     def y_scatter_copy(row, d, h):
@@ -435,12 +435,12 @@
 
     def y_scatter(row):
         for h in range(len(row_halves)):
-            for d in (1, 3, 2):
+            for d in (2, 1, 3):
                 y_scatter_copy(row, d, h).start()
 
     def y_total(row, h):
         cut = row_halves[h]
-        for d in (1, 3, 2):
+        for d in (2, 1, 3):
             y_scatter_copy(row, d, h).wait()
         total = y_send[shard, cut].astype(F32)
         for d in (1, 2, 3):
@@ -453,12 +453,12 @@
 
     def spread_half(row, buffer, h, block):
         buffer[p, row_halves[h]] = block
-        for d in (1, 3, 2):
+        for d in (2, 1, 3):
             spread_copy(row, buffer, d, h).start()
 
     def wait_spread(row, buffer):
         for h in range(len(row_halves)):
-            for d in (1, 3, 2):
+            for d in (2, 1, 3):
                 spread_copy(row, buffer, d, h).wait()
 
     column_halves = (pl.ds(0, width // 2), pl.ds(width // 2, width // 2))
@@ -472,7 +472,7 @@
                 target.at[layer, f, h, d],
                 q_device(d),
             )
-            for d in (1, 3, 2)
+            for d in (2, 1, 3)
         ]
 
     def choose_all(layer, f, h):
@@ -509,7 +509,7 @@
                 if gated:
                     block = block * share
                 block = block.astype(BF16)
-                for d in (1, 3, 2):
+                for d in (2, 1, 3):
                     packed_send[f, h, d - 1, :, cut] = block[
                         d * part_rows : (d + 1) * part_rows
                     ]
@@ -528,13 +528,13 @@
                 target.at[f, h, d],
                 q_device(-d),
             )
-            for d in (1, 3, 2)
+            for d in (2, 1, 3)
         ]
 
     def put_result(row, f, h, send, target, columns):
         for cut in column_halves:
             block = columns(cut).astype(BF16)
-            for d in (1, 3, 2):
+            for d in (2, 1, 3):
                 send[f, h, d - 1, :, cut] = block[d * part_rows : (d + 1) * part_rows]
             target[f, h, 0, :, cut] = block[:part_rows]
         for copy in result_copies(row, f, h, send, target):
@@ -568,12 +568,12 @@
 
     def start_partials(row, target):
         for h in range(len(row_halves)):
-            for d in (1, 3, 2):
+            for d in (2, 1, 3):
                 partial_copy(row, target, d, h).start()
 
     def total_of_partials(row, target, h):
         cut = row_halves[h]
-        for d in (1, 3, 2):
+        for d in (2, 1, 3):
             partial_copy(row, target, d, h).wait()
         total = partial_send[p, cut].astype(F32)
         for d in (1, 2, 3):
@@ -605,7 +605,7 @@
 
     def attention(layer):
         for h in range(len(row_halves)):
-            for d in (1, 3, 2):
+            for d in (2, 1, 3):
                 y_gather_copy(Y_GATHER, d, h, attn_all, layer).wait()
         whole = attn_all[layer].reshape(span, width)
         raw_qk[layer] = dot(whole, weight_of(layer, 0, 0, 6))
@@ -788,23 +788,23 @@
 
         lax.fori_loop(0, RING * RING, step, 0)
         for i in range(RING):
-            for d in (1, 3, 2):
+            for d in (2, 1, 3):
                 proj_first(d, i).start()
 
     def proj_two(layer):
         for i in range(RING):
-            for d in (1, 3, 2):
+            for d in (2, 1, 3):
                 proj_first(d, i).wait()
             total = proj[core, place_of(i, p)].astype(F32)
             for d in (1, 2, 3):
                 total = total + proj_recv[d - 1, i].astype(F32)
             proj_sum[i] = total.astype(BF16)
-        for d in (1, 3, 2):
+        for d in (2, 1, 3):
             proj_second(layer, d).start()
 
     def proj_three(layer):
         total = proj_sum[q].astype(F32)
-        for d in (1, 3, 2):
+        for d in (2, 1, 3):
             proj_second(layer, d).wait()
         for d in (1, 2, 3):
             total = total + proj_last[layer, d - 1].astype(F32)
@@ -1118,7 +1118,7 @@
             ring_copy(
                 row, d, terms_recv.at[axis, 0], terms_recv.at[axis, d], device(d)
             )
-            for d in (1, 3, 2)
+            for d in (2, 1, 3)
         ]
         for copy in copies:
             copy.start()

time: 218 us -> 215 us (0.986)
  Pallas kernels: 217 us -> 214 us
    pallas_call x1, Pallas kernels: 213 us -> 210 us  [shards(): pl.pallas_call(functools.partial(kernel, rows, width, hidden, capacity),...]
where the time goes in v3:
time: 215 us
  Pallas kernels  214 us (100%)
    pallas_call x1, Pallas kernels, shards(): pl.pallas_call(functools.partial(kernel, rows, width, hidden, capacity),...  210 us

profile of v3, /device:TPU:0, one launch (start us, length us, event | category | flops | bytes accessed | tf_op | source)
XLA Modules:
  0.0 215.1 jit_solution(5068616971707536496)
XLA Ops:
  0.7 210.3 %layers.1 = (bf16[2,64,1024]{2,1,0:T(8,128)(2,1)}, f32[8,1024]{1,0:T(8,128)}, f32[2,64,384]{2,1,0:T(8,128)}, f32[3,2,128,1024]{3,2,1,0:T(8,128)}) custom-call(bf16[2,64,1024]{2,1,0:T(8,128)(2,1)} %bitcast.20, s32[2,256]{1,0:T(2,128)} %segments_ref.1, s32[2,8,64]{2,1,0:T(8,128)} %bitcast.26, f32[2,8,64]{2,1,0:T(8,128)} %bitcast.27, f32[1,1024]{1,0:T(1,128)} %attn_gain_ref.1, ...), custom_call_target="tpu_custom_call" | custom-call | flops 60000002048 | bytes 20000000 | tf_op jit(solution)/shard_map/layers/pallas_call | solution.py:1344
  211.0 3.9 %finish.1 = (bf16[1,2,64,1024]{3,2,1,0:T(8,128)(2,1)}, f32[1,1024]{1,0:T(1,128)}, f32[1,64]{1,0:T(1,128)}, f32[1,64]{1,0:T(1,128)}, f32[1,1024]{1,0:T(1,128)}, /...) custom-call(bf16[2,64,1024]{2,1,0:T(8,128)(2,1)} %get-tuple-element., ...), custom_call_target="tpu_custom_call" | custom-call | tf_op jit(solution)/shard_map/finish/pallas_call | solution.py:1393

commit v4 on v3

--- a/solution.py
+++ b/solution.py
@@ -26,8 +26,8 @@
 PACKED, PACKED_BACK, RESULT, RESULT_BACK, RING_ROWS = 40, 44, 48, 52, 56
 
 C_ENDS, C_GAINS, C_ROUTES, C_GATES, C_PIECE = range(5)
-C_GATE, C_UP, C_DOWN, C_GRAD, C_PROJ, C_TERM, C_OUT_ENDS = 5, 6, 7, 8, 11, 12, 13
-C_OUT_EXPERT, C_OUT_PROJ, CORE_ROWS = 14, 20, 22
+C_GATE, C_UP, C_DOWN, C_GRAD, C_TERM, C_OUT_ENDS = 5, 6, 7, 8, 12, 13
+C_OUT_EXPERT, C_OUT_PROJ, C_PROJ, CORE_ROWS = 14, 20, 22, 26
 
 
 def dot(a, b, form=NN):
@@ -754,8 +754,9 @@
             lax.fori_loop(0, 4, step, 0)
             grad_core(kind).start()
 
-    def proj_core_copy():
-        return core_copy(C_PROJ, proj.at[other], proj_core)
+    def proj_core_copy(i):
+        at = pl.ds(RING * i, RING)
+        return core_copy(C_PROJ + i, proj.at[other, at], proj_core.at[at])
 
     def proj_first(d, i):
         return pltpu.make_async_remote_copy(
@@ -780,13 +781,13 @@
         return core_copy(C_OUT_PROJ + layer, proj_stage, proj_out.at[core])
 
     def proj_one():
-        proj_core_copy().wait()
-
         def step(i, _):
-            proj[core, i] = (proj[core, i].astype(F32) + proj_core[i].astype(F32)).astype(BF16)
+            proj_core_copy(i).wait()
+            at = pl.ds(RING * i, RING)
+            proj[core, at] = (proj[core, at].astype(F32) + proj_core[at].astype(F32)).astype(BF16)
             return 0
 
-        lax.fori_loop(0, RING * RING, step, 0)
+        lax.fori_loop(0, RING, step, 0)
         for i in range(RING):
             for d in (2, 1, 3):
                 proj_first(d, i).start()
@@ -912,10 +913,10 @@
                 proj[half, at, :, start * HEAD : stop * HEAD] = change.reshape(
                     4, rows, (stop - start) * HEAD
                 )
+            proj_core_copy(i).start()
             return 0
 
         lax.fori_loop(0, 4, step, 0)
-        proj_core_copy().start()
 
     def finish_back(layer, take):
         for h, cut in enumerate(row_halves):

time: 215 us -> 215 us (level)
  no operation moved by 1% of the time
where the time goes in v4:
time: 215 us
  Pallas kernels  214 us (100%)
    pallas_call x1, Pallas kernels, shards(): pl.pallas_call(functools.partial(kernel, rows, width, hidden, capacity),...  210 us

profile of v4, /device:TPU:0, one launch (start us, length us, event | category | flops | bytes accessed | tf_op | source)
XLA Modules:
  0.0 215.0 jit_solution(3867486453824334452)
XLA Ops:
  0.7 210.3 %layers.1 = (bf16[2,64,1024]{2,1,0:T(8,128)(2,1)}, f32[8,1024]{1,0:T(8,128)}, f32[2,64,384]{2,1,0:T(8,128)}, f32[3,2,128,1024]{3,2,1,0:T(8,128)}) custom-call(bf16[2,64,1024]{2,1,0:T(8,128)(2,1)} %bitcast.20, s32[2,256]{1,0:T(2,128)} %segments_ref.1, s32[2,8,64]{2,1,0:T(8,128)} %bitcast.26, f32[2,8,64]{2,1,0:T(8,128)} %bitcast.27, f32[1,1024]{1,0:T(1,128)} %attn_gain_ref.1, ...), custom_call_target="tpu_custom_call" | custom-call | flops 60000002048 | bytes 20000000 | tf_op jit(solution)/shard_map/layers/pallas_call | solution.py:1345
  211.0 3.9 %finish.1 = (bf16[1,2,64,1024]{3,2,1,0:T(8,128)(2,1)}, f32[1,1024]{1,0:T(1,128)}, f32[1,64]{1,0:T(1,128)}, f32[1,64]{1,0:T(1,128)}, f32[1,1024]{1,0:T(1,128)}, /...) custom-call(bf16[2,64,1024]{2,1,0:T(8,128)(2,1)} %get-tuple-element., ...), custom_call_target="tpu_custom_call" | custom-call | tf_op jit(solution)/shard_map/finish/pallas_call | solution.py:1394
